TPU v7x, 32 devices: a whole 2x2x4 slice. The times are simulated.
32 devices in a mesh: grp: 2 (over x), col: 16 (over z, y, core).
Axes of the slice: x: 2, y: 2, z: 4, core: 2. Of those that a mesh axis runs over, the one named last changes fastest.
Arguments:
- database: int32 [256, 4096], P('col', 'grp'), parts along dimension 1, may hold values from 0 to 255
- queries: int32 [16, 256], P('grp', 'col'), parts along dimension 0, may hold values from -2147483648 to 2147483646
- key_rows: int32 [16, 8192], P('grp', 'col'), parts along dimension 0, may hold values from -2147483648 to 2147483646
- hint: int32 [4, 1024], P('grp'), parts along dimension 0, may hold values from -2147483648 to 2147483646
- assignment: int32 [32], P('grp'), parts along dimension 0, may hold values from 0 to 15, each once
Outputs:
- packed: float32 [32, 2, 1024], P(('grp', 'col')), parts along dimension 0
There are 2 independent parts, one for each index of `grp`. A program takes and returns all parts, laid end to end along the dimension named above; each array names one. Nothing has to cross between parts.
Inputs may be any that keep to these rules, and one draw needn't show every extreme that they name: `assignment`: every unit appears in exactly one slot.
All inputs are finite; a program needn't handle non-finite values.
Results may differ from a plain program's by a relative error of at most 0.0003.
Values sent between devices are 32-bit elements; how exact they have to be, the bound alone decides.
No kernel may reach another device: no remote copies, remote signals or barrier semaphores. Data moves between devices by JAX's collectives and lax.ppermute only.
A program may use at most 128 MiB of HBM per device.

v0:
```python
import jax
import jax.numpy as jnp
from jax import lax
from jax.sharding import PartitionSpec as P

LEVELS = 2
DIGITS = 2


def automorph(polynomial, galois):
    cycle_width = polynomial.shape[0]
    inverse = pow(galois, -1, 2 * cycle_width)
    source = jnp.arange(cycle_width, dtype=jnp.int32) * inverse % (2 * cycle_width)
    picked = jnp.take(polynomial, source % cycle_width, axis=0)
    return jnp.where(source < cycle_width, picked, -picked)


def toeplitz(key_poly):
    cycle_width = key_poly.shape[0]
    shifted = jnp.concatenate([-key_poly[1:], key_poly, -key_poly[:1]])
    tiled_rows = jnp.tile(shifted, cycle_width)[: cycle_width * (2 * cycle_width - 1)]
    return tiled_rows.reshape(cycle_width, 2 * cycle_width - 1)[
        :, cycle_width - 1 : 2 * cycle_width - 1
    ]


def switch_section(mask_poly, value_poly, section_keys, galois):
    cycle_width = mask_poly.shape[0]
    rotated_mask = automorph(mask_poly, galois)
    rotated_value = automorph(value_poly, galois)
    switched = jnp.zeros((2 * cycle_width,), jnp.int32)
    for digit_index in range(section_keys.shape[0]):
        digit_row = jnp.bitwise_and(jnp.right_shift(rotated_mask, 16 * digit_index), 65535)
        matrix = jnp.concatenate(
            [toeplitz(section_keys[digit_index, 0]), toeplitz(section_keys[digit_index, 1])], axis=1
        )
        switched = (
            switched + jnp.dot(digit_row[None, :], matrix, preferred_element_type=jnp.int32)[0]
        )
    return (mask_poly + switched[:cycle_width], value_poly + rotated_value + switched[cycle_width:])


def pack_unit(mask_poly, value_poly, key_row):
    cycle_width = mask_poly.shape[0]
    section_table = key_row.reshape(LEVELS, DIGITS, 2, cycle_width)
    for section_index in range(LEVELS):
        galois = cycle_width // 2**section_index + 1
        mask_poly, value_poly = switch_section(
            mask_poly, value_poly, section_table[section_index], galois
        )
    return jnp.stack([mask_poly, value_poly])


def split_words(words):
    lower_half = jnp.bitwise_and(words, 65535).astype(jnp.float32)
    upper_half = jnp.bitwise_and(jnp.right_shift(words, 16), 65535).astype(jnp.float32)
    return (lower_half, upper_half)


def join_words(lower_half, upper_half):
    return lower_half.astype(jnp.int32) + jnp.left_shift(upper_half.astype(jnp.int32), 16)


def on_device(database, queries, key_rows, hint, assignment):
    cycle_width = hint.shape[1]
    poly_count = hint.shape[0]
    slot_count = assignment.shape[0] // lax.axis_size("col")
    key_table = lax.all_gather(key_rows, "col", axis=1, tiled=True)
    partial_value = jnp.dot(queries, database, preferred_element_type=jnp.int32)
    owned_slots = lax.dynamic_slice_in_dim(
        assignment, lax.axis_index("col") * slot_count, slot_count
    )
    lower_half, upper_half = split_words(partial_value)
    lower_sum, upper_sum = lax.psum((lower_half, upper_half), "col")
    summed = join_words(lower_sum, upper_sum)
    value_rows = jnp.take(summed.reshape(-1, cycle_width), owned_slots, axis=0)

    def pack_one(inputs):
        unit_index, value_poly = inputs
        client = unit_index // poly_count
        poly_index = unit_index % poly_count
        mask_poly = lax.dynamic_index_in_dim(hint, poly_index, 0, keepdims=False)
        key_row = lax.dynamic_index_in_dim(key_table, client, 0, keepdims=False)
        return pack_unit(mask_poly, value_poly, key_row)

    packed_words = lax.map(pack_one, (owned_slots, value_rows))
    return packed_words.astype(jnp.float32) * 2.0 ** (-32)


def solution(mesh):
    placed = (P("col", "grp"), P("grp", "col"), P("grp", "col"), P("grp", None), P("grp"))
    return jax.shard_map(
        on_device,
        mesh=mesh,
        in_specs=placed,
        out_specs=P(("grp", "col"), None, None),
        check_vma=False,
    )
```

profile of v0, /device:TPU:0, one launch (start us, length us, event | category | flops | bytes accessed | tf_op | source)
XLA Modules:
  0.0 325.9 jit_solution(6749545963673076256)
XLA Ops:
  7.4 1.6 and_convert_fusion.1
  9.1 1.2 dynamic_slice.19
  12.9 24.2 %all_gather.3 = s32[8,8192]{1,0:T(8,128)S(1)} all-gather(s32[8,512]{1,0:T(8,128)} %param.9), channel_id=1, replica_groups=mesh['grp'=2,'col'=16] {'col'}, dimensions={1}, use_global_device_ids=true | all-gather | bytes 278528 | tf_op jit(solution)/shard_map/all_gather | solution.py:68
  40.4 2.0 copy.8
  42.4 3.8 %slice.292 = s32[2096128]{0:T(1024)} slice(s32[2097152]{0:T(1024)S(1)} %bitcast.75), slice={[0:2096128]} | slice | bytes 16769024 | tf_op jit(solution)/shard_map/while/body/eval_jaxpr/slice | solution.py:21
  46.2 12.3 %reshape.150 = s32[1024,2047]{1,0:T(8,128)} reshape(s32[2096128]{0:T(1024)} %slice.292) | data formatting | bytes 16769024 | tf_op jit(solution)/shard_map/while/body/eval_jaxpr/reshape | solution.py:22
  58.5 5.5 %slice.293 = s32[1024,1024]{1,0:T(8,128)} slice(s32[1024,2047]{1,0:T(8,128)} %reshape.150), slice={[0:1024], [1023:2047]} | slice | bytes 8388608 | tf_op jit(solution)/shard_map/while/body/eval_jaxpr/slice | solution.py:22
  65.9 2.0 copy.9
  67.9 3.7 %slice.297 = s32[2096128]{0:T(1024)} slice(s32[2097152]{0:T(1024)S(1)} %bitcast.76), slice={[0:2096128]} | slice | bytes 16769024 | tf_op jit(solution)/shard_map/while/body/eval_jaxpr/slice | solution.py:21
  71.6 12.3 %reshape.151 = s32[1024,2047]{1,0:T(8,128)} reshape(s32[2096128]{0:T(1024)} %slice.297) | data formatting | bytes 16769024 | tf_op jit(solution)/shard_map/while/body/eval_jaxpr/reshape | solution.py:22
  84.0 5.5 %slice.298 = s32[1024,1024]{1,0:T(8,128)} slice(s32[1024,2047]{1,0:T(8,128)} %reshape.151), slice={[0:1024], [1023:2047]} | slice | bytes 8388608 | tf_op jit(solution)/shard_map/while/body/eval_jaxpr/slice | solution.py:22
  89.5 4.5 %gather_fusion = s32[1024]{0:T(1024)S(1)} fusion(s32[1024]{0:T(1024)S(1)} %bitcast.69, s32[1024]{0:T(1024)S(1)} %broadcast_clamp_fusion.1), kind=kCustom, calls=%fused_computation.clone | custom fusion | bytes 12288 | tf_op jit(solution)/shard_map/while/body/eval_jaxpr/jit(_take)/gather | solution.py:14
  95.7 2.0 copy.6
  97.7 4.0 %slice.282 = s32[2096128]{0:T(1024)} slice(s32[2097152]{0:T(1024)S(1)} %bitcast.77), slice={[0:2096128]} | slice | bytes 16769024 | tf_op jit(solution)/shard_map/while/body/eval_jaxpr/slice | solution.py:21
  101.7 12.3 %reshape.148 = s32[1024,2047]{1,0:T(8,128)} reshape(s32[2096128]{0:T(1024)} %slice.282) | data formatting | bytes 16769024 | tf_op jit(solution)/shard_map/while/body/eval_jaxpr/reshape | solution.py:22
  114.0 5.4 %slice.283 = s32[1024,1024]{1,0:T(8,128)} slice(s32[1024,2047]{1,0:T(8,128)} %reshape.148), slice={[0:1024], [1023:2047]} | slice | bytes 8388608 | tf_op jit(solution)/shard_map/while/body/eval_jaxpr/slice | solution.py:22
  121.2 2.0 copy.7
  123.2 3.7 %slice.287 = s32[2096128]{0:T(1024)} slice(s32[2097152]{0:T(1024)S(1)} %bitcast.78), slice={[0:2096128]} | slice | bytes 16769024 | tf_op jit(solution)/shard_map/while/body/eval_jaxpr/slice | solution.py:21
  126.9 12.3 %reshape.149 = s32[1024,2047]{1,0:T(8,128)} reshape(s32[2096128]{0:T(1024)} %slice.287) | data formatting | bytes 16769024 | tf_op jit(solution)/shard_map/while/body/eval_jaxpr/reshape | solution.py:22
  139.2 5.4 %slice.288 = s32[1024,1024]{1,0:T(8,128)} slice(s32[1024,2047]{1,0:T(8,128)} %reshape.149), slice={[0:1024], [1023:2047]} | slice | bytes 8388608 | tf_op jit(solution)/shard_map/while/body/eval_jaxpr/slice | solution.py:22
  145.3 4.3 %broadcast_bitcast_fusion.1 = s32[128,16,8,128]{3,2,1,0:T(8,128)} fusion(s32[2048]{0:T(1024)S(1)} %concatenate.64), kind=kLoop, calls=%fused_computation.21 | loop fusion | bytes 8396800
  150.3 4.3 %broadcast_bitcast_fusion = s32[128,16,8,128]{3,2,1,0:T(8,128)} fusion(s32[2048]{0:T(1024)S(1)} %concatenate.65), kind=kLoop, calls=%fused_computation.20 | loop fusion | bytes 8396800
  155.4 4.3 %broadcast_bitcast_fusion.3 = s32[128,16,8,128]{3,2,1,0:T(8,128)} fusion(s32[2048]{0:T(1024)S(1)} %concatenate.61), kind=kLoop, calls=%fused_computation.23 | loop fusion | bytes 8396800
  160.4 5.3 %broadcast_bitcast_fusion.2 = s32[128,16,8,128]{3,2,1,0:T(8,128)} fusion(s32[2048]{0:T(1024)S(1)} %concatenate.62), kind=kLoop, calls=%fused_computation.22 | loop fusion | bytes 8396800
  165.7 1.2 copy-done.3
  166.8 7.0 %fusion.4 = s32[1,2048]{1,0:T(1,128)S(1)} fusion(s32[1024,1]{0,1:T(1,128)S(1)} %bitcast.88, s32[1024,1024]{1,0:T(8,128)S(1)} %copy-done.3, s32[1024,1024]{1,0:T(8,128)S(1)} %copy-done.2), kind=kOutput, calls=%fused_computation.8 | convolution fusion | flops 6291456 | bytes 8400896 | tf_op jit(solution)/shard_map/while/body/eval_jaxpr/dot_general | solution.py:38
  173.9 6.8 %fusion = s32[1,2048]{1,0:T(1,128)S(1)} fusion(s32[1024,1]{0,1:T(1,128)S(1)} %bitcast.87, s32[1024,1024]{1,0:T(8,128)S(1)} %copy-done.7, s32[1024,1024]{1,0:T(8,128)S(1)} %copy-done.4), kind=kOutput, calls=%fused_computation.4 | convolution fusion | flops 6291456 | bytes 8400896 | tf_op jit(solution)/shard_map/while/body/eval_jaxpr/dot_general | solution.py:38
  182.6 2.4 copy.12
  185.0 3.5 %slice.313 = s32[2096128]{0:T(1024)} slice(s32[2097152]{0:T(1024)S(1)} %bitcast.79), slice={[0:2096128]} | slice | bytes 16769024 | tf_op jit(solution)/shard_map/while/body/eval_jaxpr/slice | solution.py:21
  188.6 12.3 %reshape.154 = s32[1024,2047]{1,0:T(8,128)} reshape(s32[2096128]{0:T(1024)} %slice.313) | data formatting | bytes 16769024 | tf_op jit(solution)/shard_map/while/body/eval_jaxpr/reshape | solution.py:22
  200.9 5.5 %slice.314 = s32[1024,1024]{1,0:T(8,128)} slice(s32[1024,2047]{1,0:T(8,128)} %reshape.154), slice={[0:1024], [1023:2047]} | slice | bytes 8388608 | tf_op jit(solution)/shard_map/while/body/eval_jaxpr/slice | solution.py:22
  206.4 5.4 %copy.13 = s32[128,16,8,128]{3,1,2,0:T(8,128)S(1)} copy(s32[128,16,8,128]{3,2,1,0:T(8,128)} %broadcast_bitcast_fusion) | data formatting | bytes 16777216
  211.8 3.7 %slice.318 = s32[2096128]{0:T(1024)} slice(s32[2097152]{0:T(1024)S(1)} %bitcast.80), slice={[0:2096128]} | slice | bytes 16769024 | tf_op jit(solution)/shard_map/while/body/eval_jaxpr/slice | solution.py:21
  215.5 12.3 %reshape.155 = s32[1024,2047]{1,0:T(8,128)} reshape(s32[2096128]{0:T(1024)} %slice.318) | data formatting | bytes 16769024 | tf_op jit(solution)/shard_map/while/body/eval_jaxpr/reshape | solution.py:22
  227.8 5.5 %slice.319 = s32[1024,1024]{1,0:T(8,128)} slice(s32[1024,2047]{1,0:T(8,128)} %reshape.155), slice={[0:1024], [1023:2047]} | slice | bytes 8388608 | tf_op jit(solution)/shard_map/while/body/eval_jaxpr/slice | solution.py:22
  233.2 5.4 %copy.10 = s32[128,16,8,128]{3,1,2,0:T(8,128)S(1)} copy(s32[128,16,8,128]{3,2,1,0:T(8,128)} %broadcast_bitcast_fusion.3) | data formatting | bytes 16777216
  238.6 3.7 %slice.303 = s32[2096128]{0:T(1024)} slice(s32[2097152]{0:T(1024)S(1)} %bitcast.81), slice={[0:2096128]} | slice | bytes 16769024 | tf_op jit(solution)/shard_map/while/body/eval_jaxpr/slice | solution.py:21
  242.3 12.3 %reshape.152 = s32[1024,2047]{1,0:T(8,128)} reshape(s32[2096128]{0:T(1024)} %slice.303) | data formatting | bytes 16769024 | tf_op jit(solution)/shard_map/while/body/eval_jaxpr/reshape | solution.py:22
  254.7 5.4 %slice.304 = s32[1024,1024]{1,0:T(8,128)} slice(s32[1024,2047]{1,0:T(8,128)} %reshape.152), slice={[0:1024], [1023:2047]} | slice | bytes 8388608 | tf_op jit(solution)/shard_map/while/body/eval_jaxpr/slice | solution.py:22
  260.1 5.4 %copy.11 = s32[128,16,8,128]{3,1,2,0:T(8,128)S(1)} copy(s32[128,16,8,128]{3,2,1,0:T(8,128)} %broadcast_bitcast_fusion.2) | data formatting | bytes 16777216
  265.5 3.7 %slice.308 = s32[2096128]{0:T(1024)} slice(s32[2097152]{0:T(1024)S(1)} %bitcast.82), slice={[0:2096128]} | slice | bytes 16769024 | tf_op jit(solution)/shard_map/while/body/eval_jaxpr/slice | solution.py:21
  269.2 12.3 %reshape.153 = s32[1024,2047]{1,0:T(8,128)} reshape(s32[2096128]{0:T(1024)} %slice.308) | data formatting | bytes 16769024 | tf_op jit(solution)/shard_map/while/body/eval_jaxpr/reshape | solution.py:22
  281.5 5.4 %slice.309 = s32[1024,1024]{1,0:T(8,128)} slice(s32[1024,2047]{1,0:T(8,128)} %reshape.153), slice={[0:1024], [1023:2047]} | slice | bytes 8388608 | tf_op jit(solution)/shard_map/while/body/eval_jaxpr/slice | solution.py:22
  287.9 4.5 %gather_fusion.2 = s32[1024]{0:T(1024)S(1)} fusion(s32[1024]{0:T(1024)S(1)} %bitcast.71, s32[1024]{0:T(1024)S(1)} %broadcast_clamp_fusion.1), kind=kCustom, calls=%fused_computation.2.clone | custom fusion | bytes 12288 | tf_op jit(solution)/shard_map/while/body/eval_jaxpr/jit(_take)/gather | solution.py:14
  292.5 4.5 %gather_fusion.3 = s32[1024]{0:T(1024)S(1)} fusion(s32[1024]{0:T(1024)S(1)} %get-tuple-element.68, s32[1024]{0:T(1024)S(1)} %get-tuple-element.73), kind=kCustom, calls=%fused_computation.3.clone | custom fusion | bytes 12288 | tf_op jit(solution)/shard_map/while/body/eval_jaxpr/jit(_take)/gather | solution.py:14
  297.0 4.5 %gather_fusion.1 = s32[1024]{0:T(1024)S(1)} fusion(s32[1024]{0:T(1024)S(1)} %get-tuple-element.67, s32[1024]{0:T(1024)S(1)} %get-tuple-element.73), kind=kCustom, calls=%fused_computation.1.clone | custom fusion | bytes 12288 | tf_op jit(solution)/shard_map/while/body/eval_jaxpr/jit(_take)/gather | solution.py:14
  301.6 9.5 %fusion.12 = s32[1,2048]{1,0:T(1,128)S(1)} fusion(s32[1024,1]{0,1:T(1,128)S(1)} %bitcast.90, s32[1024,1024]{1,0:T(8,128)} %slice.319, s32[1024,1024]{1,0:T(8,128)} %slice.314), kind=kOutput, calls=%fused_computation.16 | convolution fusion | flops 6291456 | bytes 8400896 | tf_op jit(solution)/shard_map/while/body/eval_jaxpr/dot_general | solution.py:38
  311.2 6.8 %fusion.8 = s32[1,2048]{1,0:T(1,128)S(1)} fusion(s32[1024,1]{0,1:T(1,128)S(1)} %bitcast.89, s32[1024,1024]{1,0:T(8,128)S(1)} %copy-done.6, s32[1024,1024]{1,0:T(8,128)S(1)} %copy-done.5), kind=kOutput, calls=%fused_computation.12 | convolution fusion | flops 6291456 | bytes 8400896 | tf_op jit(solution)/shard_map/while/body/eval_jaxpr/dot_general | solution.py:38
  (58 shorter events, 9.0 us)
Async XLA Ops:
  6.5 0.9 copy-start
  6.5 280.5 %all-reduce.3.cloned.1.call-start = ((), (), s32[]{:S(2)}) async-start(), calls=%async_computation | async-start | bytes 262144 | tf_op jit(solution)/shard_map/psum | solution.py:74
  84.0 5.5 %copy-start.8 = (s32[2,1024]{1,0:T(2,128)S(1)}, s32[2,1024]{1,0:T(2,128)}, u32[]{:S(2)}) copy-start(s32[2,1024]{1,0:T(2,128)} %param.10) | copy-start | bytes 24580
  160.4 5.3 %copy-start.2 = (s32[1024,1024]{1,0:T(8,128)S(1)}, s32[1024,1024]{1,0:T(8,128)}, u32[]{:S(2)}) copy-start(s32[1024,1024]{1,0:T(8,128)} %slice.293) | copy-start | bytes 12582916
  160.4 6.5 %copy-start.3 = (s32[1024,1024]{1,0:T(8,128)S(1)}, s32[1024,1024]{1,0:T(8,128)}, u32[]{:S(2)}) copy-start(s32[1024,1024]{1,0:T(8,128)} %slice.298) | copy-start | bytes 12582916
  160.4 13.5 %copy-start.4 = (s32[1024,1024]{1,0:T(8,128)S(1)}, s32[1024,1024]{1,0:T(8,128)}, u32[]{:S(2)}) copy-start(s32[1024,1024]{1,0:T(8,128)} %slice.283) | copy-start | bytes 12582916
  160.4 13.5 %copy-start.7 = (s32[1024,1024]{1,0:T(8,128)S(1)}, s32[1024,1024]{1,0:T(8,128)}, u32[]{:S(2)}) copy-start(s32[1024,1024]{1,0:T(8,128)} %slice.288) | copy-start | bytes 12582916
  166.8 15.7 %slice-start = ((s8[8388608]{0:T(1024)(128)(4,1)}), s8[4194304]{0:T(1024)(128)(4,1)S(1)}, s32[]{:S(2)}) async-start(s8[8388608]{0:T(1024)(128)(4,1)} %bitcast.73), calls=%async_computation.1 | async-start | bytes 8388608
  173.8 8.7 %slice-start.1 = ((s8[8388608]{0:T(1024)(128)(4,1)}), s8[4194304]{0:T(1024)(128)(4,1)S(1)}, s32[]{:S(2)}) async-start(s8[8388608]{0:T(1024)(128)(4,1)} %bitcast.73), calls=%async_computation.2 | async-start | bytes 8388608
  301.6 9.6 %copy-start.5 = (s32[1024,1024]{1,0:T(8,128)S(1)}, s32[1024,1024]{1,0:T(8,128)}, u32[]{:S(2)}) copy-start(s32[1024,1024]{1,0:T(8,128)} %slice.304) | copy-start | bytes 12582916
  301.6 9.6 %copy-start.6 = (s32[1024,1024]{1,0:T(8,128)S(1)}, s32[1024,1024]{1,0:T(8,128)}, u32[]{:S(2)}) copy-start(s32[1024,1024]{1,0:T(8,128)} %slice.309) | copy-start | bytes 12582916
  301.6 17.0 %copy-start.1 = (s32[16,2048]{1,0:T(8,128)S(1)}, s32[16,2048]{1,0:T(8,128)}, u32[]{:S(2)}) copy-start(s32[16,2048]{1,0:T(8,128)} %param.7) | copy-start | bytes 393220
Sparse Core Ops, SparseCore 0:
  10.9 89.9 all-reduce.2
where the time goes:
time: 330 us; the launch traced here: 326 us
  local copies, waits for them, and re-layouts  244 us (74%)
  matrix products  31.6 us (10%)
  blocking collectives  24.2 us (7%)
  between operations  23.8 us (7%)
    reshape x8, local copies, waits for them, and re-layouts, toeplitz(): tiled_rows.reshape(cycle_width, 2 * cycle_width - 1)  98.5 us
    unnamed x38, local copies, waits for them, and re-layouts  51 us
    slice x8, local copies, waits for them, and re-layouts, toeplitz(): tiled_rows.reshape(cycle_width, 2 * cycle_width - 1)  43.7 us
    dot_general x4, matrix products, switch_section(): jnp.dot(digit_row[None, :], matrix, preferred_element_type=jnp.int32)[0]  30 us
    slice x8, local copies, waits for them, and re-layouts, toeplitz(): jnp.tile(shifted, cycle_width)[:cycle_width * (2 * cycle_width - 1)]  29.8 us
    all_gather x1, blocking collectives, on_device(): key_table = lax.all_gather(key_rows, 'col', axis=1, tiled=True)  24.2 us
    gather x4, local copies, waits for them, and re-layouts, automorph(): picked = jnp.take(polynomial, source % cycle_width, axis=0)  18.1 us
  transfers between devices with their start and end apart: 1, of which 0 were waited for; matrix products, arithmetic and copies ran while one was open for 74% of the time, Pallas kernels for 0%

commit v1 on v0

v1 whole, which is shorter than its diff:
```python
import functools

import jax
import jax.numpy as jnp
from jax import lax
from jax.experimental import pallas as pl
from jax.experimental.pallas import tpu as pltpu
from jax.sharding import PartitionSpec as P

LEVELS = 2
DIGITS = 2
LANES = 128
DEPTH = 64


def step_masks(n):
    return [1] + [(1 << k) | 1 for k in range(1, n.bit_length() - 1)]


def row_masks(masks):
    rows = [0]
    for mask in reversed(masks):
        rows = rows + [r ^ mask for r in rows]
    return rows


def answer_kernel(n, polys, assignment, database, queries, key_rows, answers_out, keys_out, rows, key_scratch):
    clients = queries.shape[0]
    blocks = database.shape[1] // LANES
    cycle_blocks = blocks // polys
    words = queries[...]
    bytes_ = [jnp.bitwise_and(jnp.right_shift(words, 8 * j), 255) for j in range(4)]
    lhs = jnp.concatenate(bytes_, axis=0).astype(jnp.float32).astype(jnp.bfloat16)
    rhs = database[...].astype(jnp.float32).astype(jnp.bfloat16)
    sums = jnp.dot(lhs, rhs, preferred_element_type=jnp.float32).astype(jnp.int32)
    partial = sums[:clients]
    for j in range(1, 4):
        partial = partial + jnp.left_shift(sums[j * clients : (j + 1) * clients], 8 * j)
    for m in range(blocks):
        rows[pl.ds(m, clients, stride=blocks), :] = partial[:, m * LANES : (m + 1) * LANES]
    me = lax.axis_index("col")
    chunk = 0
    if keys_out is not None:
        chunk = key_rows.shape[1] // LANES
        for m in range(chunk):
            key_scratch[pl.ds(m, clients, stride=chunk), :] = key_rows[:, m * LANES : (m + 1) * LANES]
    for r, mask in enumerate(row_masks(step_masks(n))):
        unit = assignment[jnp.bitwise_xor(me, mask)]
        answers_out[r * cycle_blocks : (r + 1) * cycle_blocks, :] = rows[
            pl.ds(pl.multiple_of(unit * cycle_blocks, cycle_blocks), cycle_blocks), :
        ]
        if keys_out is not None:
            keys_out[r * chunk : (r + 1) * chunk, :] = key_scratch[pl.ds(unit // polys * chunk, chunk), :]


def shift_blocks(poly, count):
    blocks = poly.shape[0]
    whole, part = divmod(count % (2 * blocks), blocks)
    if part:
        row = lax.broadcasted_iota(jnp.int32, poly.shape, 0)
        poly = pltpu.roll(poly, part, 0)
        poly = jnp.where(row < part, -poly, poly)
    return -poly if whole else poly


def automorph(poly, level):
    blocks, lanes = poly.shape
    lane = lax.broadcasted_iota(jnp.int32, poly.shape, 1)
    period = 2 ** (level + 1)
    residue = jnp.bitwise_and(lane, period - 1)
    result = poly
    for m in range(1, period):
        result = jnp.where(residue == m, shift_blocks(poly, m * blocks // 2**level), result)
    return result


def toeplitz(word):
    blocks = word.shape[0]
    row = lax.broadcasted_iota(jnp.int32, (DEPTH, LANES), 0)
    lane = lax.broadcasted_iota(jnp.int32, (DEPTH, LANES), 1)
    inside = lane >= row
    turned = [
        pltpu.roll(jnp.broadcast_to(word[b : b + 1, :], (DEPTH, LANES)), 0, 1, stride=1, stride_axis=0)
        for b in range(blocks)
    ]
    columns = []
    for b in range(blocks):
        words = jnp.where(inside, turned[b], turned[b - 1])
        parts = []
        for j in range(4):
            part = jnp.bitwise_and(jnp.right_shift(words, 8 * j), 255).astype(jnp.float32)
            if b == 0:
                part = jnp.where(inside, part, -part)
            parts.append(part.astype(jnp.bfloat16))
        columns.append(jnp.concatenate(parts, axis=0))
    return jnp.concatenate(columns, axis=1)


def key_matrix(keys):
    lane = lax.broadcasted_iota(jnp.int32, keys[0][0].shape, 1)
    low = lane < DEPTH
    halves = [[None] * DIGITS for _ in range(4)]
    for p in range(2):
        for t in range(DIGITS):
            word = keys[t][p]
            other = pltpu.roll(word, DEPTH, 1)
            halves[2 * p][t] = jnp.where(low, word, jnp.left_shift(other, 8))
            halves[2 * p + 1][t] = jnp.where(low, other, jnp.left_shift(word, 8))
    rows = []
    for p in range(2):
        for s in range(4):
            for h in range(2):
                cut = [jnp.bitwise_and(jnp.right_shift(halves[2 * p + h][t], 8 * s), 255) for t in range(DIGITS)]
                rows.append(jnp.concatenate(cut, axis=1))
    return jnp.concatenate(rows, axis=0).astype(jnp.float32).astype(jnp.bfloat16)


def switch(keys, word):
    blocks = word.shape[0]
    sums = jnp.dot(key_matrix(keys), toeplitz(word), preferred_element_type=jnp.float32).astype(jnp.int32)
    lane = lax.broadcasted_iota(jnp.int32, word.shape, 1)
    results = []
    for p in range(2):
        halves = []
        for h in range(2):
            total = None
            for m in range(blocks):
                joined = None
                for s in range(4):
                    first = ((p * 4 + s) * 2 + h) * blocks
                    piece = jnp.left_shift(sums[first : first + blocks, m * LANES : (m + 1) * LANES], 8 * s)
                    joined = piece if joined is None else joined + piece
                moved = shift_blocks(joined, m)
                total = moved if total is None else total + moved
            halves.append(total)
        turned = pltpu.roll(halves[1], DEPTH, 1)
        results.append(halves[0] + jnp.where(lane < DEPTH, shift_blocks(turned, 1), turned))
    return results


def pack_kernel(n, polys, assignment, hint, answers, key_chunks, packed, keys):
    me = lax.axis_index("col")
    cycle_blocks = answers.shape[0]
    unit = assignment[me]
    mask = hint[unit % polys]
    value = answers[...]
    if len(key_chunks.shape) == 3:
        chunk = key_chunks.shape[1]
        order = row_masks(step_masks(n))
        for source in range(n):
            away = jnp.bitwise_xor(me, source)
            parity = away
            k = 1
            while k < n.bit_length():
                parity = jnp.bitwise_xor(parity, jnp.right_shift(parity, k))
                k *= 2
            slot = jnp.bitwise_or(jnp.bitwise_and(away, n - 2), jnp.bitwise_and(parity, 1))
            keys[source * chunk : (source + 1) * chunk, :] = key_chunks[slot]
    else:
        keys[...] = key_chunks[...]
    for level in range(LEVELS):
        table = [
            [keys[pl.ds(((level * DIGITS + t) * 2 + p) * cycle_blocks, cycle_blocks), :] for p in range(2)]
            for t in range(DIGITS)
        ]
        change = switch(table, automorph(mask, level))
        mask = mask + change[0]
        value = value + automorph(value, level) + change[1]
    for p, words in enumerate((mask, value)):
        scaled = words.astype(jnp.float32) * 2.0**-32
        for b in range(cycle_blocks):
            packed[0, p : p + 1, b * LANES : (b + 1) * LANES] = scaled[b : b + 1, :]


def on_device(database, queries, key_rows, hint, assignment):
    n = lax.axis_size("col")
    polys, cycle_width = hint.shape
    clients = queries.shape[0]
    cycle_blocks = cycle_width // LANES
    key_width = key_rows.shape[1]
    whole_rows = key_width % LANES == 0
    me = lax.axis_index("col")
    masks = step_masks(n)
    vmem = pl.BlockSpec(memory_space=pltpu.VMEM)
    smem = pl.BlockSpec(memory_space=pltpu.SMEM)
    chunk = key_width // LANES

    out_shape = [jax.ShapeDtypeStruct((n * cycle_blocks, LANES), jnp.int32)]
    if whole_rows:
        out_shape.append(jax.ShapeDtypeStruct((n * chunk, LANES), jnp.int32))

        def first_kernel(*refs):
            answer_kernel(n, polys, *refs)
    else:

        def first_kernel(assignment, database, queries, key_rows, answers_out, rows, key_scratch):
            answer_kernel(n, polys, assignment, database, queries, key_rows, answers_out, None, rows, key_scratch)

    outs = pl.pallas_call(
        first_kernel,
        out_shape=out_shape,
        in_specs=[smem, vmem, vmem, vmem],
        out_specs=[vmem] * len(out_shape),
        scratch_shapes=[
            pltpu.VMEM((clients * polys * cycle_blocks, LANES), jnp.int32),
            pltpu.VMEM((clients * max(chunk, 1), LANES), jnp.int32),
        ],
    )(assignment, database, queries, key_rows)
    answers = outs[0].reshape(n, cycle_blocks, LANES)
    if whole_rows:
        keys = outs[1].reshape(1, n, chunk, LANES)
    else:
        order = jnp.bitwise_xor(jnp.array(row_masks(masks), jnp.int32), me)
        keys = jnp.take(key_rows, assignment[order] // polys, axis=0).reshape(1, n, 1, key_width)

    rows = n
    for mask in masks:
        half = rows // 2
        sent = jnp.concatenate(
            [answers[half:].reshape(-1, LANES), keys[:, half:].reshape(-1, LANES)], axis=0
        )
        got = lax.ppermute(sent, "col", [(i, i ^ mask) for i in range(n)])
        answers = answers[:half] + got[: half * cycle_blocks].reshape(half, cycle_blocks, LANES)
        kept = keys[:, :half]
        keys = jnp.concatenate([kept, got[half * cycle_blocks :].reshape(kept.shape)], axis=0)
        rows = half

    answers = answers.reshape(cycle_blocks, LANES)
    if whole_rows:
        keys = keys.reshape(n, chunk, LANES)
    else:
        away = jnp.bitwise_xor(jnp.arange(n, dtype=jnp.int32), me)
        parity = away
        k = 1
        while k < n.bit_length():
            parity = jnp.bitwise_xor(parity, jnp.right_shift(parity, k))
            k *= 2
        slot = jnp.bitwise_or(jnp.bitwise_and(away, n - 2), jnp.bitwise_and(parity, 1))
        keys = jnp.take(keys.reshape(n, key_width), slot, axis=0).reshape(-1, LANES)

    return pl.pallas_call(
        functools.partial(pack_kernel, n, polys),
        out_shape=jax.ShapeDtypeStruct((1, 2, cycle_width), jnp.float32),
        in_specs=[smem, vmem, vmem, vmem],
        out_specs=vmem,
        scratch_shapes=[pltpu.VMEM((LEVELS * DIGITS * 2 * cycle_blocks, LANES), jnp.int32)],
    )(assignment, hint.reshape(polys, cycle_blocks, LANES), answers, keys)


def solution(mesh):
    placed = (P("col", "grp"), P("grp", "col"), P("grp", "col"), P("grp", None), P("grp"))
    return jax.shard_map(
        on_device,
        mesh=mesh,
        in_specs=placed,
        out_specs=P(("grp", "col"), None, None),
        check_vma=False,
    )
```

time: 330 us -> 22.6 us (0.07); the launches traced: 326 us -> 22.2 us
  local copies, waits for them, and re-layouts: 244 us -> 4.14 us
  matrix products: 31.6 us -> 0 us
  blocking collectives: 24.2 us -> 0 us
  between operations: 23.8 us -> 0.07 us
  starting transfers between devices: 0.01 us -> 7.77 us
  waiting for transfers between devices: 0.02 us -> 4.89 us
  Pallas kernels: 0 us -> 4.08 us
    reshape x9 -> x0, local copies, waits for them, and re-layouts: 98.6 us -> none  [the longest x8 98.5 us: toeplitz(): tiled_rows.reshape(cycle_width, 2 * cycle_width - 1)]
    slice x21 -> x12, local copies, waits for them, and re-layouts: 74.9 us -> 2.17 us  [the longest x6 1.38 us: on_device(): answers[half:].reshape(-1, LANES)]
    unnamed x38 -> x13, local copies, waits for them, and re-layouts: 51 us -> 1.97 us
    dot_general x5 -> x0, matrix products: 31.6 us -> none  [the longest x4 30 us: switch_section(): jnp.dot(digit_row[None, :], matrix, preferred_element_type=jnp.int32)[0]]
    all_gather x1 -> x0, blocking collectives: 24.2 us -> none  [on_device(): key_table = lax.all_gather(key_rows, 'col', axis=1, tiled=True)]
    gather x4 -> x0, local copies, waits for them, and re-layouts: 18.1 us -> none  [automorph(): picked = jnp.take(polynomial, source % cycle_width, axis=0)]
    ppermute x0 -> x4, starting transfers between devices: none -> 7.77 us  [on_device(): got = lax.ppermute(sent, 'col', [(i, i ^ mask) for i in range(n)])]
    ppermute x0 -> x4, waiting for transfers between devices: none -> 4.89 us  [on_device(): got = lax.ppermute(sent, 'col', [(i, i ^ mask) for i in range(n)])]
  transfers between devices with their start and end apart: 1 -> 4, of which waited for: 0 -> 4; matrix products, arithmetic and copies ran while one was open for 74% -> 3% of each run, Pallas kernels for 0% -> 0%
where the time goes in v1:
time: 22.6 us; the launch traced here: 22.2 us
  starting transfers between devices  7.77 us (34%)
  waiting for transfers between devices  4.89 us (22%)
  local copies, waits for them, and re-layouts  4.14 us (18%)
  Pallas kernels  4.08 us (18%)
  other arithmetic  1.26 us (6%)
    ppermute x4, starting transfers between devices, on_device(): got = lax.ppermute(sent, 'col', [(i, i ^ mask) for i in range(n)])  7.77 us
    ppermute x4, waiting for transfers between devices, on_device(): got = lax.ppermute(sent, 'col', [(i, i ^ mask) for i in range(n)])  4.89 us
    pallas_call x1, Pallas kernels, on_device(): pl.pallas_call(functools.partial(pack_kernel, n, polys), out_shape=jax.Sh...  2.33 us
    unnamed x13, local copies, waits for them, and re-layouts  1.97 us
    pallas_call x1, Pallas kernels, on_device(): pl.pallas_call(first_kernel, out_shape=out_shape, in_specs=[smem, vmem, v...  1.75 us
    slice x6, local copies, waits for them, and re-layouts, on_device(): answers[half:].reshape(-1, LANES)  1.38 us
    slice x3, local copies, waits for them, and re-layouts, on_device(): keys[:, half:].reshape(-1, LANES)  0.78 us
    reshape x1, other arithmetic, on_device(): keys = keys.reshape(n, chunk, LANES)  0.61 us
  transfers between devices with their start and end apart: 4, of which 4 were waited for; matrix products, arithmetic and copies ran while one was open for 3% of the time, Pallas kernels for 0%

profile of v1, /device:TPU:0, one launch (start us, length us, event | category | flops | bytes accessed | tf_op | source)
XLA Modules:
  0.0 22.2 jit_solution(5499057893394704059)
XLA Ops:
  0.0 1.8 %shard_map.55 = (s32[128,128]{1,0:T(8,128)}, s32[64,128]{1,0:T(8,128)}) custom-call(s32[16]{0:T(128)} %assignment.1, s32[16,2048]{1,0:T(8,128)} %refs_1_.1, s32[8,16]{1,0:T(8,128)} %refs_2_.1, s32[8,512]{1,0:T(8,128)} %refs_3_.1), custom_call_target="tpu_custom_call" | custom-call | tf_op jit(solution)/shard_map/pallas_call | solution.py:199
  1.8 0.0 copy-start.2
  1.8 0.8 %fusion.3 = (s32[1,8,4,128]{3,2,0,1:T(4,128)S(1)}, s32[1,8,4,128]{3,2,0,1:T(4,128)S(1)}) fusion(s32[1,16,4,128]{3,2,0,1:T(4,128)} %bitcast.23), kind=kLoop, calls=%fused_computation.22 | loop fusion | bytes 65536 | tf_op jit(solution)/shard_map/slice | solution.py:220
  2.5 0.1 copy-done.2
  2.6 0.5 %collective-permute-start = (s32[96,128]{1,0:T(8,128)S(1)}, s32[96,128]{1,0:T(8,128)S(1)}, u32[]{:S(2)}, u32[]{:S(2)}) collective-permute-start(s32[96,128]{1,0:T(8,128)S(1)} %pad_add_fusion), channel_id=1, source_target_pairs={{0,1},{1,0},{2,3},{3,2},{4,5},{5,4},{6,7},{7,6},{8,9},{9,8},{10,11... | collective-permute-start | bytes 147464 | tf_op jit(solution)/shard_map/ppermute | solution.py:222
  3.1 0.9 %collective-permute-done = s32[96,128]{1,0:T(8,128)S(1)} collective-permute-done((s32[96,128]{1,0:T(8,128)S(1)}, s32[96,128]{1,0:T(8,128)S(1)}, u32[]{:S(2)}, u32[]{:S(2)}) %collective-permute-start) | collective-permute-done | bytes 49184 | tf_op jit(solution)/shard_map/ppermute | solution.py:222
  4.0 0.0 copy-start
  4.0 0.6 %copy-done = s32[64,128]{1,0:T(8,128)} copy-done((s32[64,128]{1,0:T(8,128)}, s32[64,128]{1,0:T(8,128)S(1)}, u32[]{:S(2)}) %copy-start) | copy-done | bytes 32792
  4.6 0.0 slice-start
  4.7 0.7 %slice-done = s32[32,128]{1,0:T(8,128)S(1)} async-done(((s32[64,128]{1,0:T(8,128)}), s32[32,128]{1,0:T(8,128)S(1)}, s32[]{:S(2)}) %slice-start) | async-done | bytes 16408 | tf_op jit(solution)/shard_map/slice | solution.py:220
  5.4 0.0 copy-start.1
  5.4 2.6 %collective-permute-start.1 = (s32[64,128]{1,0:T(8,128)S(1)}, s32[64,128]{1,0:T(8,128)S(1)}, u32[]{:S(2)}, u32[]{:S(2)}) collective-permute-start(s32[64,128]{1,0:T(8,128)S(1)} %pad_add_fusion.1), channel_id=1, source_target_pairs={{0,3},{1,2},{2,1},{3,0},{4,7},{5,6},{6,5},{7,4},{8,11},{9,10},{10,... | collective-permute-start | bytes 98312 | tf_op jit(solution)/shard_map/ppermute | solution.py:222
  8.0 1.6 %collective-permute-done.1 = s32[64,128]{1,0:T(8,128)S(1)} collective-permute-done((s32[64,128]{1,0:T(8,128)S(1)}, s32[64,128]{1,0:T(8,128)S(1)}, u32[]{:S(2)}, u32[]{:S(2)}) %collective-permute-start.1) | collective-permute-done | bytes 32800 | tf_op jit(solution)/shard_map/ppermute | solution.py:222
  9.6 0.0 copy-done.1
  9.6 1.9 %collective-permute-start.2 = (s32[48,128]{1,0:T(8,128)S(1)}, s32[48,128]{1,0:T(8,128)S(1)}, u32[]{:S(2)}, u32[]{:S(2)}) collective-permute-start(s32[48,128]{1,0:T(8,128)S(1)} %pad_add_fusion.2), channel_id=1, source_target_pairs={{0,5},{1,4},{2,7},{3,6},{4,1},{5,0},{6,3},{7,2},{8,13},{9,12},{10,... | collective-permute-start | bytes 73736 | tf_op jit(solution)/shard_map/ppermute | solution.py:222
  11.5 1.5 %collective-permute-done.2 = s32[48,128]{1,0:T(8,128)S(1)} collective-permute-done((s32[48,128]{1,0:T(8,128)S(1)}, s32[48,128]{1,0:T(8,128)S(1)}, u32[]{:S(2)}, u32[]{:S(2)}) %collective-permute-start.2) | collective-permute-done | bytes 24608 | tf_op jit(solution)/shard_map/ppermute | solution.py:222
  13.0 0.0 copy-start.3
  13.0 0.6 %copy-done.3 = s32[16,128]{1,0:T(8,128)} copy-done((s32[16,128]{1,0:T(8,128)}, s32[16,128]{1,0:T(8,128)S(1)}, u32[]{:S(2)}) %copy-start.3) | copy-done | bytes 8216
  13.6 0.0 slice-start.1
  13.7 0.7 %slice-done.1 = s32[8,128]{1,0:T(8,128)S(1)} async-done(((s32[16,128]{1,0:T(8,128)}), s32[8,128]{1,0:T(8,128)S(1)}, s32[]{:S(2)}) %slice-start.1) | async-done | bytes 4120 | tf_op jit(solution)/shard_map/slice | solution.py:220
  14.3 0.0 copy-start.5
  14.3 2.7 %collective-permute-start.3 = (s32[40,128]{1,0:T(8,128)S(1)}, s32[40,128]{1,0:T(8,128)S(1)}, u32[]{:S(2)}, u32[]{:S(2)}) collective-permute-start(s32[40,128]{1,0:T(8,128)S(1)} %pad_add_fusion.3), channel_id=1, source_target_pairs={{0,9},{1,8},{2,11},{3,10},{4,13},{5,12},{6,15},{7,14},{8,1},{9,0},... | collective-permute-start | bytes 61448 | tf_op jit(solution)/shard_map/ppermute | solution.py:222
  17.1 0.0 copy-done.5
  17.1 0.6 %copy.16 = s32[1,2,8,128]{3,2,1,0:T(8,128)} copy(s32[1,2,8,128]{3,1,2,0:T(2,128)S(1)} %bitcast.25) | data formatting | bytes 16384
  17.7 0.9 %collective-permute-done.3 = s32[40,128]{1,0:T(8,128)S(1)} collective-permute-done((s32[40,128]{1,0:T(8,128)S(1)}, s32[40,128]{1,0:T(8,128)S(1)}, u32[]{:S(2)}, u32[]{:S(2)}) %collective-permute-start.3) | collective-permute-done | bytes 20512 | tf_op jit(solution)/shard_map/ppermute | solution.py:222
  18.6 0.0 copy-start.4
  18.6 0.6 %add_bitcast_fusion.key_chunks = s32[16,4,128]{2,1,0:T(4,128)} fusion(s32[8,1,4,128]{3,2,0,1:T(4,128)S(1)} %bitcast.21, s32[8,1,4,128]{3,2,0,1:T(4,128)S(1)} %get-tuple-element.9), kind=kLoop, calls=%fused_computation.9 | loop fusion | flops 8192 | bytes 65536 | tf_op jit(solution)/shard_map/reshape | solution.py:230
  19.2 0.1 copy-done.4
  19.3 0.6 %slice_add_fusion.3.answers = s32[8,128]{1,0:T(8,128)} fusion(s32[40,128]{1,0:T(8,128)S(1)} %collective-permute-done.3, s32[16,128]{1,0:T(8,128)S(1)} %copy-done.4), kind=kLoop, calls=%fused_computation.21 | loop fusion | flops 1024 | bytes 12288 | tf_op jit(solution)/shard_map/add | solution.py:223
  19.9 2.3 %shard_map.56 = f32[1,2,1024]{2,1,0:T(2,128)} custom-call(s32[16]{0:T(128)} %assignment.1, s32[2,8,128]{2,1,0:T(8,128)} %bitcast.24, s32[8,128]{1,0:T(8,128)} %slice_add_fusion.3.answers, s32[16,4,128]{2,1,0:T(4,128)} %add_bitcast_fusion.key_chunks), custom_call_target="tpu_custom_call" | custom-call | tf_op jit(solution)/shard_map/pallas_call | solution.py:241
  (17 shorter events, 0.1 us)
Async XLA Ops:
  1.8 0.8 %copy-start.2 = (s32[128,128]{1,0:T(8,128)S(1)}, s32[128,128]{1,0:T(8,128)}, u32[]{:S(2)}) copy-start(s32[128,128]{1,0:T(8,128)} %get-tuple-element.7) | copy-start | bytes 196612
  2.6 1.4 %collective-permute-start = (s32[96,128]{1,0:T(8,128)S(1)}, s32[96,128]{1,0:T(8,128)S(1)}, u32[]{:S(2)}, u32[]{:S(2)}) collective-permute-start(s32[96,128]{1,0:T(8,128)S(1)} %pad_add_fusion), channel_id=1, source_target_pairs={{0,1},{1,0},{2,3},{3,2},{4,5},{5,4},{6,7},{7,6},{8,9},{9,8},{10,11... | collective-permute-start | bytes 147464 | tf_op jit(solution)/shard_map/ppermute | solution.py:222
  4.0 0.6 %copy-start = (s32[64,128]{1,0:T(8,128)}, s32[64,128]{1,0:T(8,128)S(1)}, u32[]{:S(2)}) copy-start(s32[64,128]{1,0:T(8,128)S(1)} %slice_add_fusion) | copy-start | bytes 98308
  4.6 0.7 %slice-start = ((s32[64,128]{1,0:T(8,128)}), s32[32,128]{1,0:T(8,128)S(1)}, s32[]{:S(2)}) async-start(s32[64,128]{1,0:T(8,128)} %copy-done), calls=%async_computation | async-start | bytes 32768 | tf_op jit(solution)/shard_map/slice | solution.py:220
  5.4 4.2 %copy-start.1 = (s32[64,128]{1,0:T(8,128)S(1)}, s32[64,128]{1,0:T(8,128)}, u32[]{:S(2)}) copy-start(s32[64,128]{1,0:T(8,128)} %copy-done) | copy-start | bytes 98308
  5.4 4.2 %collective-permute-start.1 = (s32[64,128]{1,0:T(8,128)S(1)}, s32[64,128]{1,0:T(8,128)S(1)}, u32[]{:S(2)}, u32[]{:S(2)}) collective-permute-start(s32[64,128]{1,0:T(8,128)S(1)} %pad_add_fusion.1), channel_id=1, source_target_pairs={{0,3},{1,2},{2,1},{3,0},{4,7},{5,6},{6,5},{7,4},{8,11},{9,10},{10,... | collective-permute-start | bytes 98312 | tf_op jit(solution)/shard_map/ppermute | solution.py:222
  9.6 3.4 %collective-permute-start.2 = (s32[48,128]{1,0:T(8,128)S(1)}, s32[48,128]{1,0:T(8,128)S(1)}, u32[]{:S(2)}, u32[]{:S(2)}) collective-permute-start(s32[48,128]{1,0:T(8,128)S(1)} %pad_add_fusion.2), channel_id=1, source_target_pairs={{0,5},{1,4},{2,7},{3,6},{4,1},{5,0},{6,3},{7,2},{8,13},{9,12},{10,... | collective-permute-start | bytes 73736 | tf_op jit(solution)/shard_map/ppermute | solution.py:222
  13.0 0.6 %copy-start.3 = (s32[16,128]{1,0:T(8,128)}, s32[16,128]{1,0:T(8,128)S(1)}, u32[]{:S(2)}) copy-start(s32[16,128]{1,0:T(8,128)S(1)} %slice_add_fusion.2) | copy-start | bytes 24580
  13.6 0.7 %slice-start.1 = ((s32[16,128]{1,0:T(8,128)}), s32[8,128]{1,0:T(8,128)S(1)}, s32[]{:S(2)}) async-start(s32[16,128]{1,0:T(8,128)} %copy-done.3), calls=%async_computation.1 | async-start | bytes 8192 | tf_op jit(solution)/shard_map/slice | solution.py:220
  14.3 2.8 %copy-start.5 = (s32[2,1024]{1,0:T(2,128)S(1)}, s32[2,1024]{1,0:T(2,128)}, u32[]{:S(2)}) copy-start(s32[2,1024]{1,0:T(2,128)} %param.8) | copy-start | bytes 24580
  14.3 4.2 %collective-permute-start.3 = (s32[40,128]{1,0:T(8,128)S(1)}, s32[40,128]{1,0:T(8,128)S(1)}, u32[]{:S(2)}, u32[]{:S(2)}) collective-permute-start(s32[40,128]{1,0:T(8,128)S(1)} %pad_add_fusion.3), channel_id=1, source_target_pairs={{0,9},{1,8},{2,11},{3,10},{4,13},{5,12},{6,15},{7,14},{8,1},{9,0},... | collective-permute-start | bytes 61448 | tf_op jit(solution)/shard_map/ppermute | solution.py:222
  18.6 0.7 %copy-start.4 = (s32[16,128]{1,0:T(8,128)S(1)}, s32[16,128]{1,0:T(8,128)}, u32[]{:S(2)}) copy-start(s32[16,128]{1,0:T(8,128)} %copy-done.3) | copy-start | bytes 24580

commit v2 on v1

v2 whole, which is shorter than its diff:
```python
import functools

import jax
import jax.numpy as jnp
from jax import lax
from jax.experimental import pallas as pl
from jax.experimental.pallas import tpu as pltpu
from jax.sharding import PartitionSpec as P

LEVELS = 2
DIGITS = 2
LANES = 128
DEPTH = 64


def step_masks(n):
    return [1] + [(1 << k) | 1 for k in range(1, n.bit_length() - 1)]


def row_masks(masks):
    rows = [0]
    for mask in reversed(masks):
        rows = rows + [r ^ mask for r in rows]
    return rows


def answer_kernel(n, polys, assignment, database, queries, key_rows, kept, sent, rows, key_scratch):
    clients = queries.shape[0]
    blocks = database.shape[1] // LANES
    cycle_blocks = blocks // polys
    words = queries[...]
    bytes_ = [jnp.bitwise_and(jnp.right_shift(words, 8 * j), 255) for j in range(4)]
    lhs = jnp.concatenate(bytes_, axis=0).astype(jnp.float32).astype(jnp.bfloat16)
    rhs = database[...].astype(jnp.float32).astype(jnp.bfloat16)
    sums = jnp.dot(lhs, rhs, preferred_element_type=jnp.float32).astype(jnp.int32)
    partial = sums[:clients]
    for j in range(1, 4):
        partial = partial + jnp.left_shift(sums[j * clients : (j + 1) * clients], 8 * j)
    for m in range(blocks):
        rows[pl.ds(m, clients, stride=blocks), :] = partial[:, m * LANES : (m + 1) * LANES]
    half = n // 2
    chunk = kept.shape[0] // half - cycle_blocks
    for m in range(chunk):
        key_scratch[pl.ds(m, clients, stride=chunk), :] = key_rows[:, m * LANES : (m + 1) * LANES]
    me = lax.axis_index("col")
    for r, mask in enumerate(row_masks(step_masks(n))):
        unit = assignment[jnp.bitwise_xor(me, mask)]
        out, place = (kept, r) if r < half else (sent, r - half)
        out[place * cycle_blocks : (place + 1) * cycle_blocks, :] = rows[
            pl.ds(pl.multiple_of(unit * cycle_blocks, cycle_blocks), cycle_blocks), :
        ]
        if chunk:
            place = half * cycle_blocks + place * chunk
            out[place : place + chunk, :] = key_scratch[pl.ds(unit // polys * chunk, chunk), :]


def join_kernel(cycle_blocks, rows, chunk, kept, got, next_kept, next_sent):
    half = rows // 2
    cut = half * cycle_blocks
    next_kept[:cut, :] = kept[:cut, :] + got[:cut, :]
    next_sent[:cut, :] = kept[cut : 2 * cut, :] + got[cut : 2 * cut, :]
    if chunk:
        sources = (kept.shape[0] - 2 * cut) // (rows * chunk)
        size = half * chunk
        for s in range(2 * sources):
            part = kept if s < sources else got
            first = 2 * cut + s % sources * 2 * size
            next_kept[cut + s * size : cut + (s + 1) * size, :] = part[first : first + size, :]
            next_sent[cut + s * size : cut + (s + 1) * size, :] = part[first + size : first + 2 * size, :]


def shift_blocks(poly, count):
    blocks = poly.shape[0]
    whole, part = divmod(count % (2 * blocks), blocks)
    if part:
        row = lax.broadcasted_iota(jnp.int32, poly.shape, 0)
        poly = pltpu.roll(poly, part, 0)
        poly = jnp.where(row < part, -poly, poly)
    return -poly if whole else poly


def automorph(poly, level):
    blocks, lanes = poly.shape
    lane = lax.broadcasted_iota(jnp.int32, poly.shape, 1)
    period = 2 ** (level + 1)
    residue = jnp.bitwise_and(lane, period - 1)
    result = poly
    for m in range(1, period):
        result = jnp.where(residue == m, shift_blocks(poly, m * blocks // 2**level), result)
    return result


def toeplitz(word):
    blocks = word.shape[0]
    row = lax.broadcasted_iota(jnp.int32, (DEPTH, LANES), 0)
    lane = lax.broadcasted_iota(jnp.int32, (DEPTH, LANES), 1)
    inside = lane >= row
    turned = [
        pltpu.roll(jnp.broadcast_to(word[b : b + 1, :], (DEPTH, LANES)), 0, 1, stride=1, stride_axis=0)
        for b in range(blocks)
    ]
    columns = []
    for b in range(blocks):
        words = jnp.where(inside, turned[b], turned[b - 1])
        parts = []
        for j in range(4):
            part = jnp.bitwise_and(jnp.right_shift(words, 8 * j), 255).astype(jnp.float32)
            if b == 0:
                part = jnp.where(inside, part, -part)
            parts.append(part.astype(jnp.bfloat16))
        columns.append(jnp.concatenate(parts, axis=0))
    return jnp.concatenate(columns, axis=1)


def key_matrix(keys):
    lane = lax.broadcasted_iota(jnp.int32, keys[0][0].shape, 1)
    low = lane < DEPTH
    halves = [[None] * DIGITS for _ in range(4)]
    for p in range(2):
        for t in range(DIGITS):
            word = keys[t][p]
            other = pltpu.roll(word, DEPTH, 1)
            halves[2 * p][t] = jnp.where(low, word, jnp.left_shift(other, 8))
            halves[2 * p + 1][t] = jnp.where(low, other, jnp.left_shift(word, 8))
    rows = []
    for p in range(2):
        for s in range(4):
            for h in range(2):
                cut = [jnp.bitwise_and(jnp.right_shift(halves[2 * p + h][t], 8 * s), 255) for t in range(DIGITS)]
                rows.append(jnp.concatenate(cut, axis=1))
    return jnp.concatenate(rows, axis=0).astype(jnp.float32).astype(jnp.bfloat16)


def switch(keys, digits, blocks):
    sums = jnp.dot(key_matrix(keys), digits, preferred_element_type=jnp.float32).astype(jnp.int32)
    lane = lax.broadcasted_iota(jnp.int32, (blocks, LANES), 1)
    results = []
    for p in range(2):
        halves = []
        for h in range(2):
            total = None
            for m in range(blocks):
                joined = None
                for s in range(4):
                    first = ((p * 4 + s) * 2 + h) * blocks
                    piece = jnp.left_shift(sums[first : first + blocks, m * LANES : (m + 1) * LANES], 8 * s)
                    joined = piece if joined is None else joined + piece
                moved = shift_blocks(joined, m)
                total = moved if total is None else total + moved
            halves.append(total)
        turned = pltpu.roll(halves[1], DEPTH, 1)
        results.append(halves[0] + jnp.where(lane < DEPTH, shift_blocks(turned, 1), turned))
    return results


def digit_kernel(polys, assignment, hint, mask_out, digits_out):
    cycle_blocks = mask_out.shape[0]
    poly = assignment[lax.axis_index("col")] % polys
    row = hint[pl.ds(poly, 1), :]
    mask = jnp.concatenate([row[:, b * LANES : (b + 1) * LANES] for b in range(cycle_blocks)], axis=0)
    mask_out[...] = mask
    digits_out[...] = toeplitz(automorph(mask, 0))


def pack_kernel(n, chunk, mask_in, digits, kept, got, *refs):
    if chunk:
        packed, stacked, keys = refs
    else:
        keys, packed = refs
    cycle_blocks = mask_in.shape[0]
    mask = mask_in[...]
    value = kept[:cycle_blocks, :] + got[:cycle_blocks, :]
    if chunk:
        stacked[: n // 2 * chunk, :] = kept[cycle_blocks:, :]
        stacked[n // 2 * chunk :, :] = got[cycle_blocks:, :]
        me = lax.axis_index("col")
        for source in range(n):
            slot = slot_of(n, jnp.bitwise_xor(me, source))
            keys[source * chunk : (source + 1) * chunk, :] = stacked[pl.ds(slot * chunk, chunk), :]
    for level in range(LEVELS):
        table = [
            [keys[pl.ds(((level * DIGITS + t) * 2 + p) * cycle_blocks, cycle_blocks), :] for p in range(2)]
            for t in range(DIGITS)
        ]
        change = switch(table, digits[...] if level == 0 else toeplitz(automorph(mask, level)), cycle_blocks)
        mask = mask + change[0]
        value = value + automorph(value, level) + change[1]
    for p, words in enumerate((mask, value)):
        scaled = words.astype(jnp.float32) * 2.0**-32
        for b in range(cycle_blocks):
            packed[0, p : p + 1, b * LANES : (b + 1) * LANES] = scaled[b : b + 1, :]


def slot_of(n, away):
    parity = away
    k = 1
    while k < n.bit_length():
        parity = jnp.bitwise_xor(parity, jnp.right_shift(parity, k))
        k *= 2
    return jnp.bitwise_or(jnp.bitwise_and(away, n - 2), jnp.bitwise_and(parity, 1))


def near(x):
    return pltpu.with_memory_space_constraint(x, pltpu.VMEM)


def on_device(database, queries, key_rows, hint, assignment):
    n = lax.axis_size("col")
    polys, cycle_width = hint.shape
    clients = queries.shape[0]
    cycle_blocks = cycle_width // LANES
    key_width = key_rows.shape[1]
    masks = step_masks(n)
    vmem = pl.BlockSpec(memory_space=pltpu.VMEM)
    smem = pl.BlockSpec(memory_space=pltpu.SMEM)
    chunk = key_width // LANES if key_width % LANES == 0 else 0
    units = clients * polys

    def exchange(x, mask):
        return lax.ppermute(x, "col", [(i, i ^ mask) for i in range(n)])

    rows = n // 2
    kept, sent = pl.pallas_call(
        functools.partial(answer_kernel, n, polys),
        out_shape=[pltpu.VMEM((rows * (cycle_blocks + chunk), LANES), jnp.int32)] * 2,
        in_specs=[smem, vmem, vmem, vmem],
        out_specs=[vmem] * 2,
        scratch_shapes=[
            pltpu.VMEM((units * cycle_blocks, LANES), jnp.int32),
            pltpu.VMEM((max(clients * chunk, 8), LANES), jnp.int32),
        ],
    )(assignment, database, queries, key_rows)
    mask_poly, digits = pl.pallas_call(
        functools.partial(digit_kernel, polys),
        out_shape=[
            pltpu.VMEM((cycle_blocks, LANES), jnp.int32),
            pltpu.VMEM((2 * DIGITS * DEPTH, cycle_width), jnp.bfloat16),
        ],
        in_specs=[smem, vmem],
        out_specs=[vmem] * 2,
    )(assignment, hint)

    for step, mask in enumerate(masks):
        got = exchange(sent, mask)
        if step < len(masks) - 1:
            half_rows = kept.shape[0] - rows // 2 * cycle_blocks if chunk else rows // 2 * cycle_blocks
            kept, sent = pl.pallas_call(
                functools.partial(join_kernel, cycle_blocks, rows, chunk),
                out_shape=[pltpu.VMEM((half_rows, LANES), jnp.int32)] * 2,
                in_specs=[vmem] * 2,
                out_specs=[vmem] * 2,
            )(near(kept), near(got))
            rows //= 2

    operands = [near(mask_poly), near(digits), near(kept), near(got)]
    if not chunk:
        me = lax.axis_index("col")
        order = jnp.bitwise_xor(jnp.array(row_masks(masks), jnp.int32), me)
        keys = jnp.take(key_rows, assignment[order] // polys, axis=0)[None]
        for mask in masks:
            half = keys.shape[1] // 2
            keys = jnp.concatenate([keys[:, :half], exchange(keys[:, half:], mask)], axis=0)
        slots = slot_of(n, jnp.bitwise_xor(jnp.arange(n, dtype=jnp.int32), me))
        operands.append(jnp.take(keys.reshape(n, key_width), slots, axis=0).reshape(-1, LANES))
    return pl.pallas_call(
        functools.partial(pack_kernel, n, chunk),
        out_shape=jax.ShapeDtypeStruct((1, 2, cycle_width), jnp.float32),
        in_specs=[vmem] * len(operands),
        out_specs=vmem,
        scratch_shapes=[pltpu.VMEM((n * chunk, LANES), jnp.int32)] * 2 if chunk else [],
    )(*operands)


def solution(mesh):
    placed = (P("col", "grp"), P("grp", "col"), P("grp", "col"), P("grp", None), P("grp"))
    return jax.shard_map(
        on_device,
        mesh=mesh,
        in_specs=placed,
        out_specs=P(("grp", "col"), None, None),
        check_vma=False,
    )
```

time: 22.6 us -> 16.1 us (0.71)
  local copies, waits for them, and re-layouts: 4.14 us -> 0 us
  other arithmetic: 1.26 us -> 0 us
  Pallas kernels: 4.08 us -> 3.51 us
  waiting for transfers between devices: 4.89 us -> 4.55 us
    slice x12 -> x0, local copies, waits for them, and re-layouts: 2.17 us -> none  [the longest x6 1.38 us: on_device(): answers[half:].reshape(-1, LANES)]
    unnamed x13 -> x0, local copies, waits for them, and re-layouts: 1.97 us -> none
    reshape x1 -> x0, other arithmetic: 0.61 us -> none  [on_device(): keys = keys.reshape(n, chunk, LANES)]
    add x4 -> x0, other arithmetic: 0.61 us -> none  [on_device(): answers[:half]]
    pallas_call x2 -> x6, Pallas kernels: 4.08 us -> 3.51 us  [the longest x1 1.44 us: on_device(): pl.pallas_call(functools.partial(pack_kernel, n, chunk), out_shape=jax.Sh...]
    ppermute x4, waiting for transfers between devices: 4.89 us -> 4.55 us  [exchange(): return lax.ppermute(x, 'col', [(i, i ^ mask) for i in range(n)])]
  transfers between devices with their start and end apart: 4 -> 4, of which waited for: 4 -> 4; matrix products, arithmetic and copies ran while one was open for 3% -> 0% of each run, Pallas kernels for 0% -> 6%
where the time goes in v2:
time: 16.1 us; the launch traced here: 15.9 us
  starting transfers between devices  7.83 us (49%)
  waiting for transfers between devices  4.55 us (28%)
  Pallas kernels  3.51 us (22%)
    ppermute x4, starting transfers between devices, exchange(): return lax.ppermute(x, 'col', [(i, i ^ mask) for i in range(n)])  7.83 us
    ppermute x4, waiting for transfers between devices, exchange(): return lax.ppermute(x, 'col', [(i, i ^ mask) for i in range(n)])  4.55 us
    pallas_call x1, Pallas kernels, on_device(): pl.pallas_call(functools.partial(pack_kernel, n, chunk), out_shape=jax.Sh...  1.44 us
    pallas_call x1, Pallas kernels, on_device(): pl.pallas_call(functools.partial(answer_kernel, n, polys), out_shape=[plt...  1.13 us
    pallas_call x1, Pallas kernels, on_device(): pl.pallas_call(functools.partial(digit_kernel, polys), out_shape=[pltpu.V...  0.92 us
  transfers between devices with their start and end apart: 4, of which 4 were waited for; matrix products, arithmetic and copies ran while one was open for 0% of the time, Pallas kernels for 6%

profile of v2, /device:TPU:0, one launch (start us, length us, event | category | flops | bytes accessed | tf_op | source)
XLA Modules:
  0.0 15.9 jit_solution(12867591229822230392)
XLA Ops:
  0.0 1.1 %shard_map.56 = (s32[96,128]{1,0:T(8,128)S(1)}, s32[96,128]{1,0:T(8,128)S(1)}) custom-call(s32[16]{0:T(128)} %assignment.3, s32[16,2048]{1,0:T(8,128)} %database.1, s32[8,16]{1,0:T(8,128)} %queries.1, s32[8,512]{1,0:T(8,128)} %key_rows.1), custom_call_target="tpu_custom_call" | custom-call | tf_op jit(solution)/shard_map/pallas_call | solution.py:223
  1.1 0.5 %collective-permute-start = (s32[96,128]{1,0:T(8,128)S(1)}, s32[96,128]{1,0:T(8,128)S(1)}, u32[]{:S(2)}, u32[]{:S(2)}) collective-permute-start(s32[96,128]{1,0:T(8,128)S(1)} %get-tuple-element.18), channel_id=1, source_target_pairs={{0,1},{1,0},{2,3},{3,2},{4,5},{5,4},{6,7},{7,6},{8,9},{9,8},{10,11... | collective-permute-start | bytes 147464 | tf_op jit(solution)/shard_map/ppermute | solution.py:220
  1.7 0.9 %collective-permute-done.got = s32[96,128]{1,0:T(8,128)S(1)} collective-permute-done((s32[96,128]{1,0:T(8,128)S(1)}, s32[96,128]{1,0:T(8,128)S(1)}, u32[]{:S(2)}, u32[]{:S(2)}) %collective-permute-start) | collective-permute-done | bytes 49184 | tf_op jit(solution)/shard_map/ppermute | solution.py:220
  2.5 2.6 %collective-permute-start.1 = (s32[64,128]{1,0:T(8,128)S(1)}, s32[64,128]{1,0:T(8,128)S(1)}, u32[]{:S(2)}, u32[]{:S(2)}) collective-permute-start(s32[64,128]{1,0:T(8,128)S(1)} %get-tuple-element.20), channel_id=1, source_target_pairs={{0,3},{1,2},{2,1},{3,0},{4,7},{5,6},{6,5},{7,4},{8,11},{9,10},{10,... | collective-permute-start | bytes 98312 | tf_op jit(solution)/shard_map/ppermute | solution.py:220
  5.2 1.6 %collective-permute-done.1.got = s32[64,128]{1,0:T(8,128)S(1)} collective-permute-done((s32[64,128]{1,0:T(8,128)S(1)}, s32[64,128]{1,0:T(8,128)S(1)}, u32[]{:S(2)}, u32[]{:S(2)}) %collective-permute-start.1) | collective-permute-done | bytes 32800 | tf_op jit(solution)/shard_map/ppermute | solution.py:220
  6.8 1.9 %collective-permute-start.2 = (s32[48,128]{1,0:T(8,128)S(1)}, s32[48,128]{1,0:T(8,128)S(1)}, u32[]{:S(2)}, u32[]{:S(2)}) collective-permute-start(s32[48,128]{1,0:T(8,128)S(1)} %get-tuple-element.22), channel_id=1, source_target_pairs={{0,5},{1,4},{2,7},{3,6},{4,1},{5,0},{6,3},{7,2},{8,13},{9,12},{10,... | collective-permute-start | bytes 73736 | tf_op jit(solution)/shard_map/ppermute | solution.py:220
  8.7 1.5 %collective-permute-done.2.got = s32[48,128]{1,0:T(8,128)S(1)} collective-permute-done((s32[48,128]{1,0:T(8,128)S(1)}, s32[48,128]{1,0:T(8,128)S(1)}, u32[]{:S(2)}, u32[]{:S(2)}) %collective-permute-start.2) | collective-permute-done | bytes 24608 | tf_op jit(solution)/shard_map/ppermute | solution.py:220
  10.2 2.8 %collective-permute-start.3 = (s32[40,128]{1,0:T(8,128)S(1)}, s32[40,128]{1,0:T(8,128)S(1)}, u32[]{:S(2)}, u32[]{:S(2)}) collective-permute-start(s32[40,128]{1,0:T(8,128)S(1)} %get-tuple-element.24), channel_id=1, source_target_pairs={{0,9},{1,8},{2,11},{3,10},{4,13},{5,12},{6,15},{7,14},{8,1},{9,0},... | collective-permute-start | bytes 61448 | tf_op jit(solution)/shard_map/ppermute | solution.py:220
  13.0 0.9 %shard_map.55 = (s32[8,128]{1,0:T(8,128)S(1)}, bf16[256,1024]{1,0:T(8,128)(2,1)S(1)}) custom-call(s32[16]{0:T(128)} %assignment.3, s32[2,1024]{1,0:T(2,128)} %hint.1), custom_call_target="tpu_custom_call" | custom-call | tf_op jit(solution)/shard_map/pallas_call | solution.py:233
  13.9 0.6 %collective-permute-done.3.got = s32[40,128]{1,0:T(8,128)S(1)} collective-permute-done((s32[40,128]{1,0:T(8,128)S(1)}, s32[40,128]{1,0:T(8,128)S(1)}, u32[]{:S(2)}, u32[]{:S(2)}) %collective-permute-start.3) | collective-permute-done | bytes 20512 | tf_op jit(solution)/shard_map/ppermute | solution.py:220
  14.5 1.4 %shard_map.60 = f32[1,2,1024]{2,1,0:T(2,128)} custom-call(s32[8,128]{1,0:T(8,128)S(1)} %get-tuple-element.15.mask_in, bf16[256,1024]{1,0:T(8,128)(2,1)S(1)} %get-tuple-element.16.digits, s32[40,128]{1,0:T(8,128)S(1)} %get-tuple-element.23.kept, s32[40,128]{1,0:T(8,128)S(1)} %collective-permute-done.3.got), custom_call_target="tpu_custom_call" | custom-call | tf_op jit(solution)/shard_map/pallas_call | solution.py:265
  (3 shorter events, 0.0 us)
Async XLA Ops:
  1.1 1.4 %collective-permute-start = (s32[96,128]{1,0:T(8,128)S(1)}, s32[96,128]{1,0:T(8,128)S(1)}, u32[]{:S(2)}, u32[]{:S(2)}) collective-permute-start(s32[96,128]{1,0:T(8,128)S(1)} %get-tuple-element.18), channel_id=1, source_target_pairs={{0,1},{1,0},{2,3},{3,2},{4,5},{5,4},{6,7},{7,6},{8,9},{9,8},{10,11... | collective-permute-start | bytes 147464 | tf_op jit(solution)/shard_map/ppermute | solution.py:220
  2.5 4.2 %collective-permute-start.1 = (s32[64,128]{1,0:T(8,128)S(1)}, s32[64,128]{1,0:T(8,128)S(1)}, u32[]{:S(2)}, u32[]{:S(2)}) collective-permute-start(s32[64,128]{1,0:T(8,128)S(1)} %get-tuple-element.20), channel_id=1, source_target_pairs={{0,3},{1,2},{2,1},{3,0},{4,7},{5,6},{6,5},{7,4},{8,11},{9,10},{10,... | collective-permute-start | bytes 98312 | tf_op jit(solution)/shard_map/ppermute | solution.py:220
  6.8 3.4 %collective-permute-start.2 = (s32[48,128]{1,0:T(8,128)S(1)}, s32[48,128]{1,0:T(8,128)S(1)}, u32[]{:S(2)}, u32[]{:S(2)}) collective-permute-start(s32[48,128]{1,0:T(8,128)S(1)} %get-tuple-element.22), channel_id=1, source_target_pairs={{0,5},{1,4},{2,7},{3,6},{4,1},{5,0},{6,3},{7,2},{8,13},{9,12},{10,... | collective-permute-start | bytes 73736 | tf_op jit(solution)/shard_map/ppermute | solution.py:220
  10.2 4.3 %collective-permute-start.3 = (s32[40,128]{1,0:T(8,128)S(1)}, s32[40,128]{1,0:T(8,128)S(1)}, u32[]{:S(2)}, u32[]{:S(2)}) collective-permute-start(s32[40,128]{1,0:T(8,128)S(1)} %get-tuple-element.24), channel_id=1, source_target_pairs={{0,9},{1,8},{2,11},{3,10},{4,13},{5,12},{6,15},{7,14},{8,1},{9,0},... | collective-permute-start | bytes 61448 | tf_op jit(solution)/shard_map/ppermute | solution.py:220

commit v3 on v2

--- a/solution.py
+++ b/solution.py
@@ -13,18 +13,25 @@
 DEPTH = 64
 
 
-def step_masks(n):
-    return [1] + [(1 << k) | 1 for k in range(1, n.bit_length() - 1)]
-
-
-def row_masks(masks):
+def stages_of(n):
+    bits = [1 << k for k in range(n.bit_length() - 1)]
+    pair = [bits[1] | bits[2] | 1, bits[2] | 1, bits[1] | 1] if len(bits) > 2 else [b | 1 for b in bits[1:2]]
+    return [[1]] + [pair] * (len(pair) > 0) + [[b | 1] for b in bits[3:]]
+
+
+def destinations(stages):
     rows = [0]
-    for mask in reversed(masks):
-        rows = rows + [r ^ mask for r in rows]
+    for stage in reversed(stages):
+        rows = [r ^ mask for mask in [0] + stage for r in rows]
     return rows
 
 
-def answer_kernel(n, polys, assignment, database, queries, key_rows, kept, sent, rows, key_scratch):
+def sources(stages):
+    return destinations(stages[::-1])
+
+
+def answer_kernel(n, polys, assignment, database, queries, key_rows, *refs):
+    outs, (rows, key_scratch) = refs[:-2], refs[-2:]
     clients = queries.shape[0]
     blocks = database.shape[1] // LANES
     cycle_blocks = blocks // polys
@@ -38,35 +45,39 @@
         partial = partial + jnp.left_shift(sums[j * clients : (j + 1) * clients], 8 * j)
     for m in range(blocks):
         rows[pl.ds(m, clients, stride=blocks), :] = partial[:, m * LANES : (m + 1) * LANES]
-    half = n // 2
-    chunk = kept.shape[0] // half - cycle_blocks
+    share = n // len(outs)
+    chunk = outs[0].shape[0] // share - cycle_blocks
     for m in range(chunk):
         key_scratch[pl.ds(m, clients, stride=chunk), :] = key_rows[:, m * LANES : (m + 1) * LANES]
     me = lax.axis_index("col")
-    for r, mask in enumerate(row_masks(step_masks(n))):
+    for r, mask in enumerate(destinations(stages_of(n))):
         unit = assignment[jnp.bitwise_xor(me, mask)]
-        out, place = (kept, r) if r < half else (sent, r - half)
+        out, place = outs[r // share], r % share
         out[place * cycle_blocks : (place + 1) * cycle_blocks, :] = rows[
             pl.ds(pl.multiple_of(unit * cycle_blocks, cycle_blocks), cycle_blocks), :
         ]
         if chunk:
-            place = half * cycle_blocks + place * chunk
-            out[place : place + chunk, :] = key_scratch[pl.ds(unit // polys * chunk, chunk), :]
-
-
-def join_kernel(cycle_blocks, rows, chunk, kept, got, next_kept, next_sent):
-    half = rows // 2
-    cut = half * cycle_blocks
-    next_kept[:cut, :] = kept[:cut, :] + got[:cut, :]
-    next_sent[:cut, :] = kept[cut : 2 * cut, :] + got[cut : 2 * cut, :]
-    if chunk:
-        sources = (kept.shape[0] - 2 * cut) // (rows * chunk)
-        size = half * chunk
-        for s in range(2 * sources):
-            part = kept if s < sources else got
-            first = 2 * cut + s % sources * 2 * size
-            next_kept[cut + s * size : cut + (s + 1) * size, :] = part[first : first + size, :]
-            next_sent[cut + s * size : cut + (s + 1) * size, :] = part[first + size : first + 2 * size, :]
+            first = share * cycle_blocks + place * chunk
+            out[first : first + chunk, :] = key_scratch[pl.ds(unit // polys * chunk, chunk), :]
+
+
+def join_kernel(cycle_blocks, rows, chunk, partners, *refs):
+    parts, outs = refs[:partners], refs[partners:]
+    share = rows // len(outs)
+    cut = rows * cycle_blocks
+    size = share * chunk
+    for o, out in enumerate(outs):
+        span = slice(o * share * cycle_blocks, (o + 1) * share * cycle_blocks)
+        total = parts[0][span, :]
+        for part in parts[1:]:
+            total = total + part[span, :]
+        out[: share * cycle_blocks, :] = total
+        if chunk:
+            stacked = (parts[0].shape[0] - cut) // (rows * chunk)
+            for s in range(stacked * partners):
+                source = cut + (s % stacked) * rows * chunk + o * size
+                target = share * cycle_blocks + s * size
+                out[target : target + size, :] = parts[s // stacked][source : source + size, :]
 
 
 def shift_blocks(poly, count):
@@ -162,21 +173,20 @@
     digits_out[...] = toeplitz(automorph(mask, 0))
 
 
-def pack_kernel(n, chunk, mask_in, digits, kept, got, *refs):
-    if chunk:
-        packed, stacked, keys = refs
-    else:
-        keys, packed = refs
+def pack_kernel(n, chunk, partners, mask_in, digits, *refs):
+    parts = refs[:partners]
+    packed, keys = refs[partners:] if chunk else refs[:partners - 1 : -1]
     cycle_blocks = mask_in.shape[0]
     mask = mask_in[...]
-    value = kept[:cycle_blocks, :] + got[:cycle_blocks, :]
+    value = parts[0][:cycle_blocks, :]
+    for part in parts[1:]:
+        value = value + part[:cycle_blocks, :]
     if chunk:
-        stacked[: n // 2 * chunk, :] = kept[cycle_blocks:, :]
-        stacked[n // 2 * chunk :, :] = got[cycle_blocks:, :]
         me = lax.axis_index("col")
-        for source in range(n):
-            slot = slot_of(n, jnp.bitwise_xor(me, source))
-            keys[source * chunk : (source + 1) * chunk, :] = stacked[pl.ds(slot * chunk, chunk), :]
+        stacked = n // partners
+        for slot, away in enumerate(sources(stages_of(n))):
+            first = cycle_blocks + slot % stacked * chunk
+            keys[pl.ds(jnp.bitwise_xor(me, away) * chunk, chunk), :] = parts[slot // stacked][first : first + chunk, :]
     for level in range(LEVELS):
         table = [
             [keys[pl.ds(((level * DIGITS + t) * 2 + p) * cycle_blocks, cycle_blocks), :] for p in range(2)]
@@ -191,15 +201,6 @@
             packed[0, p : p + 1, b * LANES : (b + 1) * LANES] = scaled[b : b + 1, :]
 
 
-def slot_of(n, away):
-    parity = away
-    k = 1
-    while k < n.bit_length():
-        parity = jnp.bitwise_xor(parity, jnp.right_shift(parity, k))
-        k *= 2
-    return jnp.bitwise_or(jnp.bitwise_and(away, n - 2), jnp.bitwise_and(parity, 1))
-
-
 def near(x):
     return pltpu.with_memory_space_constraint(x, pltpu.VMEM)
 
@@ -210,23 +211,23 @@
     clients = queries.shape[0]
     cycle_blocks = cycle_width // LANES
     key_width = key_rows.shape[1]
-    masks = step_masks(n)
+    stages = stages_of(n)
     vmem = pl.BlockSpec(memory_space=pltpu.VMEM)
     smem = pl.BlockSpec(memory_space=pltpu.SMEM)
     chunk = key_width // LANES if key_width % LANES == 0 else 0
-    units = clients * polys
 
     def exchange(x, mask):
         return lax.ppermute(x, "col", [(i, i ^ mask) for i in range(n)])
 
-    rows = n // 2
-    kept, sent = pl.pallas_call(
+    pieces = len(stages[0]) + 1
+    rows = n // pieces
+    parts = pl.pallas_call(
         functools.partial(answer_kernel, n, polys),
-        out_shape=[pltpu.VMEM((rows * (cycle_blocks + chunk), LANES), jnp.int32)] * 2,
+        out_shape=[pltpu.VMEM((rows * (cycle_blocks + chunk), LANES), jnp.int32)] * pieces,
         in_specs=[smem, vmem, vmem, vmem],
-        out_specs=[vmem] * 2,
+        out_specs=[vmem] * pieces,
         scratch_shapes=[
-            pltpu.VMEM((units * cycle_blocks, LANES), jnp.int32),
+            pltpu.VMEM((clients * polys * cycle_blocks, LANES), jnp.int32),
             pltpu.VMEM((max(clients * chunk, 8), LANES), jnp.int32),
         ],
     )(assignment, database, queries, key_rows)
@@ -240,34 +241,39 @@
         out_specs=[vmem] * 2,
     )(assignment, hint)
 
-    for step, mask in enumerate(masks):
-        got = exchange(sent, mask)
-        if step < len(masks) - 1:
-            half_rows = kept.shape[0] - rows // 2 * cycle_blocks if chunk else rows // 2 * cycle_blocks
-            kept, sent = pl.pallas_call(
-                functools.partial(join_kernel, cycle_blocks, rows, chunk),
-                out_shape=[pltpu.VMEM((half_rows, LANES), jnp.int32)] * 2,
-                in_specs=[vmem] * 2,
-                out_specs=[vmem] * 2,
-            )(near(kept), near(got))
-            rows //= 2
-
-    operands = [near(mask_poly), near(digits), near(kept), near(got)]
+    stacked = 1
+    for step, stage in enumerate(stages):
+        parts = [parts[0]] + [exchange(part, mask) for part, mask in zip(parts[1:], stage)]
+        stacked *= len(parts)
+        if step < len(stages) - 1:
+            pieces = len(stages[step + 1]) + 1
+            share = rows // pieces
+            parts = pl.pallas_call(
+                functools.partial(join_kernel, cycle_blocks, rows, chunk, len(parts)),
+                out_shape=[pltpu.VMEM((share * (cycle_blocks + stacked * chunk), LANES), jnp.int32)] * pieces,
+                in_specs=[vmem] * len(parts),
+                out_specs=[vmem] * pieces,
+            )(*map(near, parts))
+            rows = share
+
+    operands = [near(x) for x in (mask_poly, digits, *parts)]
     if not chunk:
         me = lax.axis_index("col")
-        order = jnp.bitwise_xor(jnp.array(row_masks(masks), jnp.int32), me)
+        order = jnp.bitwise_xor(jnp.array(destinations(stages), jnp.int32), me)
         keys = jnp.take(key_rows, assignment[order] // polys, axis=0)[None]
-        for mask in masks:
-            half = keys.shape[1] // 2
-            keys = jnp.concatenate([keys[:, :half], exchange(keys[:, half:], mask)], axis=0)
-        slots = slot_of(n, jnp.bitwise_xor(jnp.arange(n, dtype=jnp.int32), me))
-        operands.append(jnp.take(keys.reshape(n, key_width), slots, axis=0).reshape(-1, LANES))
+        for stage in stages:
+            cuts = jnp.split(keys, len(stage) + 1, axis=1)
+            keys = jnp.concatenate([cuts[0]] + [exchange(x, mask) for x, mask in zip(cuts[1:], stage)], axis=0)
+        away = sources(stages)
+        places = jnp.array([away.index(i) for i in range(n)], jnp.int32)
+        places = places[jnp.bitwise_xor(jnp.arange(n, dtype=jnp.int32), me)]
+        operands.append(jnp.take(keys.reshape(n, key_width), places, axis=0).reshape(-1, LANES))
     return pl.pallas_call(
-        functools.partial(pack_kernel, n, chunk),
+        functools.partial(pack_kernel, n, chunk, len(parts)),
         out_shape=jax.ShapeDtypeStruct((1, 2, cycle_width), jnp.float32),
         in_specs=[vmem] * len(operands),
         out_specs=vmem,
-        scratch_shapes=[pltpu.VMEM((n * chunk, LANES), jnp.int32)] * 2 if chunk else [],
+        scratch_shapes=[pltpu.VMEM((n * chunk, LANES), jnp.int32)] if chunk else [],
     )(*operands)
 
 

time: 16.1 us -> 15.6 us (0.969)
  starting transfers between devices: 7.83 us -> 7.21 us
  waiting for transfers between devices: 4.55 us -> 4.72 us
    ppermute x4 -> x5, starting transfers between devices: 7.83 us -> 7.21 us  [exchange(): return lax.ppermute(x, 'col', [(i, i ^ mask) for i in range(n)])]
    ppermute x4 -> x5, waiting for transfers between devices: 4.55 us -> 4.72 us  [exchange(): return lax.ppermute(x, 'col', [(i, i ^ mask) for i in range(n)])]
    pallas_call x4 -> x3, Pallas kernels: 1.46 us -> 1.45 us  [the longest x1 1.43 us: on_device(): pl.pallas_call(functools.partial(pack_kernel, n, chunk, len(parts)), out_...]
  transfers between devices with their start and end apart: 4 -> 5, of which waited for: 4 -> 5; matrix products, arithmetic and copies ran while one was open for 0% -> 0% of each run, Pallas kernels for 6% -> 6%
where the time goes in v3:
time: 15.6 us; the launch traced here: 15.5 us
  starting transfers between devices  7.21 us (46%)
  waiting for transfers between devices  4.72 us (30%)
  Pallas kernels  3.5 us (22%)
    ppermute x5, starting transfers between devices, exchange(): return lax.ppermute(x, 'col', [(i, i ^ mask) for i in range(n)])  7.21 us
    ppermute x5, waiting for transfers between devices, exchange(): return lax.ppermute(x, 'col', [(i, i ^ mask) for i in range(n)])  4.72 us
    pallas_call x1, Pallas kernels, on_device(): pl.pallas_call(functools.partial(pack_kernel, n, chunk, len(parts)), out_...  1.43 us
    pallas_call x1, Pallas kernels, on_device(): pl.pallas_call(functools.partial(answer_kernel, n, polys), out_shape=[plt...  1.13 us
    pallas_call x1, Pallas kernels, on_device(): pl.pallas_call(functools.partial(digit_kernel, polys), out_shape=[pltpu.V...  0.92 us
  transfers between devices with their start and end apart: 5, of which 5 were waited for; matrix products, arithmetic and copies ran while one was open for 0% of the time, Pallas kernels for 6%

profile of v3, /device:TPU:0, one launch (start us, length us, event | category | flops | bytes accessed | tf_op | source)
XLA Modules:
  0.0 15.5 jit_solution(2730056254774886608)
XLA Ops:
  0.0 1.1 %shard_map.56 = (s32[96,128]{1,0:T(8,128)S(1)}, s32[96,128]{1,0:T(8,128)S(1)}) custom-call(s32[16]{0:T(128)} %assignment.3, s32[16,2048]{1,0:T(8,128)} %database.1, s32[8,16]{1,0:T(8,128)} %queries.1, s32[8,512]{1,0:T(8,128)} %key_rows.1), custom_call_target="tpu_custom_call" | custom-call | tf_op jit(solution)/shard_map/pallas_call | solution.py:224
  1.1 0.5 %collective-permute-start = (s32[96,128]{1,0:T(8,128)S(1)}, s32[96,128]{1,0:T(8,128)S(1)}, u32[]{:S(2)}, u32[]{:S(2)}) collective-permute-start(s32[96,128]{1,0:T(8,128)S(1)} %get-tuple-element.18), channel_id=1, source_target_pairs={{0,1},{1,0},{2,3},{3,2},{4,5},{5,4},{6,7},{7,6},{8,9},{9,8},{10,11... | collective-permute-start | bytes 147464 | tf_op jit(solution)/shard_map/ppermute | solution.py:220
  1.7 0.9 %collective-permute-done.refs_1_ = s32[96,128]{1,0:T(8,128)S(1)} collective-permute-done((s32[96,128]{1,0:T(8,128)S(1)}, s32[96,128]{1,0:T(8,128)S(1)}, u32[]{:S(2)}, u32[]{:S(2)}) %collective-permute-start) | collective-permute-done | bytes 49184 | tf_op jit(solution)/shard_map/ppermute | solution.py:220
  2.5 3.6 %collective-permute-start.1 = (s32[32,128]{1,0:T(8,128)S(1)}, s32[32,128]{1,0:T(8,128)S(1)}, u32[]{:S(2)}, u32[]{:S(2)}) collective-permute-start(s32[32,128]{1,0:T(8,128)S(1)} %get-tuple-element.20), channel_id=1, source_target_pairs={{0,7},{1,6},{2,5},{3,4},{4,3},{5,2},{6,1},{7,0},{8,15},{9,14},{10,... | collective-permute-start | bytes 49160 | tf_op jit(solution)/shard_map/ppermute | solution.py:220
  6.2 0.5 %collective-permute-start.2 = (s32[32,128]{1,0:T(8,128)S(1)}, s32[32,128]{1,0:T(8,128)S(1)}, u32[]{:S(2)}, u32[]{:S(2)}) collective-permute-start(s32[32,128]{1,0:T(8,128)S(1)} %get-tuple-element.21), channel_id=1, source_target_pairs={{0,5},{1,4},{2,7},{3,6},{4,1},{5,0},{6,3},{7,2},{8,13},{9,12},{10,... | collective-permute-start | bytes 49160 | tf_op jit(solution)/shard_map/ppermute | solution.py:220
  6.7 0.2 %collective-permute-start.3 = (s32[32,128]{1,0:T(8,128)S(1)}, s32[32,128]{1,0:T(8,128)S(1)}, u32[]{:S(2)}, u32[]{:S(2)}) collective-permute-start(s32[32,128]{1,0:T(8,128)S(1)} %get-tuple-element.22), channel_id=1, source_target_pairs={{0,3},{1,2},{2,1},{3,0},{4,7},{5,6},{6,5},{7,4},{8,11},{9,10},{10,... | collective-permute-start | bytes 49160 | tf_op jit(solution)/shard_map/ppermute | solution.py:220
  6.9 0.8 %collective-permute-done.1.refs_1_ = s32[32,128]{1,0:T(8,128)S(1)} collective-permute-done((s32[32,128]{1,0:T(8,128)S(1)}, s32[32,128]{1,0:T(8,128)S(1)}, u32[]{:S(2)}, u32[]{:S(2)}) %collective-permute-start.1) | collective-permute-done | bytes 16416 | tf_op jit(solution)/shard_map/ppermute | solution.py:220
  7.6 1.7 %collective-permute-done.2.refs_2_ = s32[32,128]{1,0:T(8,128)S(1)} collective-permute-done((s32[32,128]{1,0:T(8,128)S(1)}, s32[32,128]{1,0:T(8,128)S(1)}, u32[]{:S(2)}, u32[]{:S(2)}) %collective-permute-start.2) | collective-permute-done | bytes 16416 | tf_op jit(solution)/shard_map/ppermute | solution.py:220
  9.3 0.5 %collective-permute-done.3.refs_3_ = s32[32,128]{1,0:T(8,128)S(1)} collective-permute-done((s32[32,128]{1,0:T(8,128)S(1)}, s32[32,128]{1,0:T(8,128)S(1)}, u32[]{:S(2)}, u32[]{:S(2)}) %collective-permute-start.3) | collective-permute-done | bytes 16416 | tf_op jit(solution)/shard_map/ppermute | solution.py:220
  9.8 2.4 %collective-permute-start.4 = (s32[40,128]{1,0:T(8,128)S(1)}, s32[40,128]{1,0:T(8,128)S(1)}, u32[]{:S(2)}, u32[]{:S(2)}) collective-permute-start(s32[40,128]{1,0:T(8,128)S(1)} %get-tuple-element.24), channel_id=1, source_target_pairs={{0,9},{1,8},{2,11},{3,10},{4,13},{5,12},{6,15},{7,14},{8,1},{9,0},... | collective-permute-start | bytes 61448 | tf_op jit(solution)/shard_map/ppermute | solution.py:220
  12.2 0.9 %shard_map.55 = (s32[8,128]{1,0:T(8,128)S(1)}, bf16[256,1024]{1,0:T(8,128)(2,1)S(1)}) custom-call(s32[16]{0:T(128)} %assignment.3, s32[2,1024]{1,0:T(2,128)} %hint.1), custom_call_target="tpu_custom_call" | custom-call | tf_op jit(solution)/shard_map/pallas_call | solution.py:234
  13.2 0.9 %collective-permute-done.4.refs_1_ = s32[40,128]{1,0:T(8,128)S(1)} collective-permute-done((s32[40,128]{1,0:T(8,128)S(1)}, s32[40,128]{1,0:T(8,128)S(1)}, u32[]{:S(2)}, u32[]{:S(2)}) %collective-permute-start.4) | collective-permute-done | bytes 20512 | tf_op jit(solution)/shard_map/ppermute | solution.py:220
  14.0 1.4 %shard_map.59 = f32[1,2,1024]{2,1,0:T(2,128)} custom-call(s32[8,128]{1,0:T(8,128)S(1)} %get-tuple-element.15.mask_in, bf16[256,1024]{1,0:T(8,128)(2,1)S(1)} %get-tuple-element.16.digits, s32[40,128]{1,0:T(8,128)S(1)} %get-tuple-element.23.refs_0_, s32[40,128]{1,0:T(8,128)S(1)} %collective-permute-done.4.refs_1_), custom_call_target="tpu_custom_call" | custom-call | tf_op jit(solution)/shard_map/pallas_call | solution.py:271
  (2 shorter events, 0.0 us)
Async XLA Ops:
  1.1 1.4 %collective-permute-start = (s32[96,128]{1,0:T(8,128)S(1)}, s32[96,128]{1,0:T(8,128)S(1)}, u32[]{:S(2)}, u32[]{:S(2)}) collective-permute-start(s32[96,128]{1,0:T(8,128)S(1)} %get-tuple-element.18), channel_id=1, source_target_pairs={{0,1},{1,0},{2,3},{3,2},{4,5},{5,4},{6,7},{7,6},{8,9},{9,8},{10,11... | collective-permute-start | bytes 147464 | tf_op jit(solution)/shard_map/ppermute | solution.py:220
  2.5 5.1 %collective-permute-start.1 = (s32[32,128]{1,0:T(8,128)S(1)}, s32[32,128]{1,0:T(8,128)S(1)}, u32[]{:S(2)}, u32[]{:S(2)}) collective-permute-start(s32[32,128]{1,0:T(8,128)S(1)} %get-tuple-element.20), channel_id=1, source_target_pairs={{0,7},{1,6},{2,5},{3,4},{4,3},{5,2},{6,1},{7,0},{8,15},{9,14},{10,... | collective-permute-start | bytes 49160 | tf_op jit(solution)/shard_map/ppermute | solution.py:220
  6.2 3.2 %collective-permute-start.2 = (s32[32,128]{1,0:T(8,128)S(1)}, s32[32,128]{1,0:T(8,128)S(1)}, u32[]{:S(2)}, u32[]{:S(2)}) collective-permute-start(s32[32,128]{1,0:T(8,128)S(1)} %get-tuple-element.21), channel_id=1, source_target_pairs={{0,5},{1,4},{2,7},{3,6},{4,1},{5,0},{6,3},{7,2},{8,13},{9,12},{10,... | collective-permute-start | bytes 49160 | tf_op jit(solution)/shard_map/ppermute | solution.py:220
  6.7 3.2 %collective-permute-start.3 = (s32[32,128]{1,0:T(8,128)S(1)}, s32[32,128]{1,0:T(8,128)S(1)}, u32[]{:S(2)}, u32[]{:S(2)}) collective-permute-start(s32[32,128]{1,0:T(8,128)S(1)} %get-tuple-element.22), channel_id=1, source_target_pairs={{0,3},{1,2},{2,1},{3,0},{4,7},{5,6},{6,5},{7,4},{8,11},{9,10},{10,... | collective-permute-start | bytes 49160 | tf_op jit(solution)/shard_map/ppermute | solution.py:220
  9.8 4.2 %collective-permute-start.4 = (s32[40,128]{1,0:T(8,128)S(1)}, s32[40,128]{1,0:T(8,128)S(1)}, u32[]{:S(2)}, u32[]{:S(2)}) collective-permute-start(s32[40,128]{1,0:T(8,128)S(1)} %get-tuple-element.24), channel_id=1, source_target_pairs={{0,9},{1,8},{2,11},{3,10},{4,13},{5,12},{6,15},{7,14},{8,1},{9,0},... | collective-permute-start | bytes 61448 | tf_op jit(solution)/shard_map/ppermute | solution.py:220

commit v4 on v3

--- a/solution.py
+++ b/solution.py
@@ -173,32 +173,86 @@
     digits_out[...] = toeplitz(automorph(mask, 0))
 
 
+def holds_first(n, stages):
+    return jnp.logical_and(lax.axis_index("col") < n // 2, stages[-1] == [n // 2 + 1])
+
+
+def key_table(keys, level, cycle_blocks):
+    return [
+        [keys[pl.ds(((level * DIGITS + t) * 2 + p) * cycle_blocks, cycle_blocks), :] for p in range(2)]
+        for t in range(DIGITS)
+    ]
+
+
+def place_keys(n, chunk, cycle_blocks, away, part, keys):
+    me = lax.axis_index("col")
+    for slot, distance in enumerate(away):
+        first = cycle_blocks + slot * chunk
+        keys[pl.ds(jnp.bitwise_xor(me, distance) * chunk, chunk), :] = part[first : first + chunk, :]
+
+
+def early_kernel(n, chunk, mask_in, digits_in, part, mask_out, change_out, digits_out, keys):
+    stages = stages_of(n)
+    early = holds_first(n, stages)
+    cycle_blocks = mask_in.shape[0]
+
+    @pl.when(early)
+    def _():
+        place_keys(n, chunk, cycle_blocks, sources(stages[:-1]), part, keys)
+        change = switch(key_table(keys, 0, cycle_blocks), digits_in[...], cycle_blocks)
+        mask = mask_in[...] + change[0]
+        mask_out[...] = mask
+        change_out[...] = change[1]
+        digits_out[...] = toeplitz(automorph(mask, 1))
+
+    @pl.when(jnp.logical_not(early))
+    def _():
+        mask_out[...] = mask_in[...]
+        change_out[...] = jnp.zeros_like(change_out)
+        digits_out[...] = digits_in[...]
+
+
 def pack_kernel(n, chunk, partners, mask_in, digits, *refs):
-    parts = refs[:partners]
-    packed, keys = refs[partners:] if chunk else refs[:partners - 1 : -1]
     cycle_blocks = mask_in.shape[0]
-    mask = mask_in[...]
+    stages = stages_of(n)
+    if chunk:
+        change_in, *parts, packed, keys = refs
+        stacked = n // partners
+        away = sources(stages)
+        for i, part in enumerate(parts):
+            place_keys(n, chunk, cycle_blocks, away[i * stacked : (i + 1) * stacked], part, keys)
+    else:
+        *parts, keys, packed = refs
+
+    def finish(level, mask, value):
+        current = digits[...]
+        while level < LEVELS:
+            change = switch(key_table(keys, level, cycle_blocks), current, cycle_blocks)
+            mask = mask + change[0]
+            value = value + automorph(value, level) + change[1]
+            level += 1
+            if level < LEVELS:
+                current = toeplitz(automorph(mask, level))
+        for p, words in enumerate((mask, value)):
+            scaled = words.astype(jnp.float32) * 2.0**-32
+            for b in range(cycle_blocks):
+                packed[0, p : p + 1, b * LANES : (b + 1) * LANES] = scaled[b : b + 1, :]
+
     value = parts[0][:cycle_blocks, :]
     for part in parts[1:]:
         value = value + part[:cycle_blocks, :]
-    if chunk:
-        me = lax.axis_index("col")
-        stacked = n // partners
-        for slot, away in enumerate(sources(stages_of(n))):
-            first = cycle_blocks + slot % stacked * chunk
-            keys[pl.ds(jnp.bitwise_xor(me, away) * chunk, chunk), :] = parts[slot // stacked][first : first + chunk, :]
-    for level in range(LEVELS):
-        table = [
-            [keys[pl.ds(((level * DIGITS + t) * 2 + p) * cycle_blocks, cycle_blocks), :] for p in range(2)]
-            for t in range(DIGITS)
-        ]
-        change = switch(table, digits[...] if level == 0 else toeplitz(automorph(mask, level)), cycle_blocks)
-        mask = mask + change[0]
-        value = value + automorph(value, level) + change[1]
-    for p, words in enumerate((mask, value)):
-        scaled = words.astype(jnp.float32) * 2.0**-32
-        for b in range(cycle_blocks):
-            packed[0, p : p + 1, b * LANES : (b + 1) * LANES] = scaled[b : b + 1, :]
+    if not chunk:
+        finish(0, mask_in[...], value)
+        return
+    early = holds_first(n, stages)
+
+    @pl.when(early)
+    def _():
+        finish(1, mask_in[...], value + automorph(value, 0) + change_in[...])
+
+    @pl.when(jnp.logical_not(early))
+    def _():
+        finish(0, mask_in[...], value)
 
 
 def near(x):
@@ -242,7 +296,17 @@
     )(assignment, hint)
 
     stacked = 1
+    extra = []
     for step, stage in enumerate(stages):
+        if chunk and step == len(stages) - 1:
+            mask_poly, change, digits = pl.pallas_call(
+                functools.partial(early_kernel, n, chunk),
+                out_shape=[pltpu.VMEM(mask_poly.shape, jnp.int32)] * 2 + [pltpu.VMEM(digits.shape, jnp.bfloat16)],
+                in_specs=[vmem] * 3,
+                out_specs=[vmem] * 3,
+                scratch_shapes=[pltpu.VMEM((n * chunk, LANES), jnp.int32)],
+            )(near(mask_poly), near(digits), near(parts[0]))
+            extra = [change]
         parts = [parts[0]] + [exchange(part, mask) for part, mask in zip(parts[1:], stage)]
         stacked *= len(parts)
         if step < len(stages) - 1:
@@ -256,7 +320,7 @@
             )(*map(near, parts))
             rows = share
 
-    operands = [near(x) for x in (mask_poly, digits, *parts)]
+    operands = [near(x) for x in (mask_poly, digits, *extra, *parts)]
     if not chunk:
         me = lax.axis_index("col")
         order = jnp.bitwise_xor(jnp.array(destinations(stages), jnp.int32), me)

time: 15.6 us -> 15.2 us (0.974)
  waiting for transfers between devices: 4.72 us -> 4.13 us
    ppermute x5, waiting for transfers between devices: 4.72 us -> 4.13 us  [exchange(): return lax.ppermute(x, 'col', [(i, i ^ mask) for i in range(n)])]
    pallas_call x0 -> x1, Pallas kernels: none -> 0.58 us  [on_device(): pl.pallas_call(functools.partial(early_kernel, n, chunk), out_shape=[pltp...]
    pallas_call x1, Pallas kernels: 1.43 us -> 0.98 us  [on_device(): pl.pallas_call(functools.partial(pack_kernel, n, chunk, len(parts)), out_...]
  transfers between devices with their start and end apart: 5 -> 5, of which waited for: 5 -> 5; matrix products, arithmetic and copies ran while one was open for 0% -> 0% of each run, Pallas kernels for 6% -> 10%
where the time goes in v4:
time: 15.2 us; the launch traced here: 15 us
  starting transfers between devices  7.21 us (47%)
  waiting for transfers between devices  4.13 us (27%)
  Pallas kernels  3.63 us (24%)
    ppermute x5, starting transfers between devices, exchange(): return lax.ppermute(x, 'col', [(i, i ^ mask) for i in range(n)])  7.21 us
    ppermute x5, waiting for transfers between devices, exchange(): return lax.ppermute(x, 'col', [(i, i ^ mask) for i in range(n)])  4.13 us
    pallas_call x1, Pallas kernels, on_device(): pl.pallas_call(functools.partial(answer_kernel, n, polys), out_shape=[plt...  1.13 us
    pallas_call x1, Pallas kernels, on_device(): pl.pallas_call(functools.partial(pack_kernel, n, chunk, len(parts)), out_...  0.98 us
    pallas_call x1, Pallas kernels, on_device(): pl.pallas_call(functools.partial(digit_kernel, polys), out_shape=[pltpu.V...  0.92 us
    pallas_call x1, Pallas kernels, on_device(): pl.pallas_call(functools.partial(early_kernel, n, chunk), out_shape=[pltp...  0.58 us
  transfers between devices with their start and end apart: 5, of which 5 were waited for; matrix products, arithmetic and copies ran while one was open for 0% of the time, Pallas kernels for 10%

profile of v4, /device:TPU:0, one launch (start us, length us, event | category | flops | bytes accessed | tf_op | source)
XLA Modules:
  0.0 15.0 jit_solution(3239960882579764503)
XLA Ops:
  0.0 1.1 %shard_map.56 = (s32[96,128]{1,0:T(8,128)S(1)}, s32[96,128]{1,0:T(8,128)S(1)}) custom-call(s32[16]{0:T(128)} %assignment.3, s32[16,2048]{1,0:T(8,128)} %database.1, s32[8,16]{1,0:T(8,128)} %queries.1, s32[8,512]{1,0:T(8,128)} %key_rows.1), custom_call_target="tpu_custom_call" | custom-call | tf_op jit(solution)/shard_map/pallas_call | solution.py:278
  1.1 0.5 %collective-permute-start = (s32[96,128]{1,0:T(8,128)S(1)}, s32[96,128]{1,0:T(8,128)S(1)}, u32[]{:S(2)}, u32[]{:S(2)}) collective-permute-start(s32[96,128]{1,0:T(8,128)S(1)} %get-tuple-element.21), channel_id=1, source_target_pairs={{0,1},{1,0},{2,3},{3,2},{4,5},{5,4},{6,7},{7,6},{8,9},{9,8},{10,11... | collective-permute-start | bytes 147464 | tf_op jit(solution)/shard_map/ppermute | solution.py:274
  1.7 0.9 %collective-permute-done.refs_1_ = s32[96,128]{1,0:T(8,128)S(1)} collective-permute-done((s32[96,128]{1,0:T(8,128)S(1)}, s32[96,128]{1,0:T(8,128)S(1)}, u32[]{:S(2)}, u32[]{:S(2)}) %collective-permute-start) | collective-permute-done | bytes 49184 | tf_op jit(solution)/shard_map/ppermute | solution.py:274
  2.5 3.6 %collective-permute-start.1 = (s32[32,128]{1,0:T(8,128)S(1)}, s32[32,128]{1,0:T(8,128)S(1)}, u32[]{:S(2)}, u32[]{:S(2)}) collective-permute-start(s32[32,128]{1,0:T(8,128)S(1)} %get-tuple-element.23), channel_id=1, source_target_pairs={{0,7},{1,6},{2,5},{3,4},{4,3},{5,2},{6,1},{7,0},{8,15},{9,14},{10,... | collective-permute-start | bytes 49160 | tf_op jit(solution)/shard_map/ppermute | solution.py:274
  6.2 0.5 %collective-permute-start.2 = (s32[32,128]{1,0:T(8,128)S(1)}, s32[32,128]{1,0:T(8,128)S(1)}, u32[]{:S(2)}, u32[]{:S(2)}) collective-permute-start(s32[32,128]{1,0:T(8,128)S(1)} %get-tuple-element.24), channel_id=1, source_target_pairs={{0,5},{1,4},{2,7},{3,6},{4,1},{5,0},{6,3},{7,2},{8,13},{9,12},{10,... | collective-permute-start | bytes 49160 | tf_op jit(solution)/shard_map/ppermute | solution.py:274
  6.7 0.2 %collective-permute-start.3 = (s32[32,128]{1,0:T(8,128)S(1)}, s32[32,128]{1,0:T(8,128)S(1)}, u32[]{:S(2)}, u32[]{:S(2)}) collective-permute-start(s32[32,128]{1,0:T(8,128)S(1)} %get-tuple-element.25), channel_id=1, source_target_pairs={{0,3},{1,2},{2,1},{3,0},{4,7},{5,6},{6,5},{7,4},{8,11},{9,10},{10,... | collective-permute-start | bytes 49160 | tf_op jit(solution)/shard_map/ppermute | solution.py:274
  6.9 0.8 %collective-permute-done.1.refs_1_ = s32[32,128]{1,0:T(8,128)S(1)} collective-permute-done((s32[32,128]{1,0:T(8,128)S(1)}, s32[32,128]{1,0:T(8,128)S(1)}, u32[]{:S(2)}, u32[]{:S(2)}) %collective-permute-start.1) | collective-permute-done | bytes 16416 | tf_op jit(solution)/shard_map/ppermute | solution.py:274
  7.6 1.7 %collective-permute-done.2.refs_2_ = s32[32,128]{1,0:T(8,128)S(1)} collective-permute-done((s32[32,128]{1,0:T(8,128)S(1)}, s32[32,128]{1,0:T(8,128)S(1)}, u32[]{:S(2)}, u32[]{:S(2)}) %collective-permute-start.2) | collective-permute-done | bytes 16416 | tf_op jit(solution)/shard_map/ppermute | solution.py:274
  9.3 0.5 %collective-permute-done.3.refs_3_ = s32[32,128]{1,0:T(8,128)S(1)} collective-permute-done((s32[32,128]{1,0:T(8,128)S(1)}, s32[32,128]{1,0:T(8,128)S(1)}, u32[]{:S(2)}, u32[]{:S(2)}) %collective-permute-start.3) | collective-permute-done | bytes 16416 | tf_op jit(solution)/shard_map/ppermute | solution.py:274
  9.8 2.4 %collective-permute-start.4 = (s32[40,128]{1,0:T(8,128)S(1)}, s32[40,128]{1,0:T(8,128)S(1)}, u32[]{:S(2)}, u32[]{:S(2)}) collective-permute-start(s32[40,128]{1,0:T(8,128)S(1)} %get-tuple-element.30), channel_id=1, source_target_pairs={{0,9},{1,8},{2,11},{3,10},{4,13},{5,12},{6,15},{7,14},{8,1},{9,0},... | collective-permute-start | bytes 61448 | tf_op jit(solution)/shard_map/ppermute | solution.py:274
  12.2 0.9 %shard_map.55 = (s32[8,128]{1,0:T(8,128)S(1)}, bf16[256,1024]{1,0:T(8,128)(2,1)S(1)}) custom-call(s32[16]{0:T(128)} %assignment.3, s32[2,1024]{1,0:T(2,128)} %hint.1), custom_call_target="tpu_custom_call" | custom-call | tf_op jit(solution)/shard_map/pallas_call | solution.py:288
  13.2 0.6 %shard_map.59 = (s32[8,128]{1,0:T(8,128)S(1)}, s32[8,128]{1,0:T(8,128)S(1)}, bf16[256,1024]{1,0:T(8,128)(2,1)S(1)}) custom-call(s32[8,128]{1,0:T(8,128)S(1)} %get-tuple-element.18.mask_in, bf16[256,1024]{1,0:T(8,128)(2,1)S(1)} %get-tuple-element.19.digits_in, s32[40,128]{1,0:T(8,128)S(1)} %get-tuple-element.26.part.refs_1_), custom_call_target="tpu_custom_call" | custom-call | tf_op jit(solution)/shard_map/pallas_call | solution.py:302
  13.7 0.3 %collective-permute-done.4.refs_2_ = s32[40,128]{1,0:T(8,128)S(1)} collective-permute-done((s32[40,128]{1,0:T(8,128)S(1)}, s32[40,128]{1,0:T(8,128)S(1)}, u32[]{:S(2)}, u32[]{:S(2)}) %collective-permute-start.4) | collective-permute-done | bytes 20512 | tf_op jit(solution)/shard_map/ppermute | solution.py:274
  14.0 1.0 %shard_map.60 = f32[1,2,1024]{2,1,0:T(2,128)} custom-call(s32[8,128]{1,0:T(8,128)S(1)} %get-tuple-element.27.mask_in, bf16[256,1024]{1,0:T(8,128)(2,1)S(1)} %get-tuple-element.28.digits, s32[8,128]{1,0:T(8,128)S(1)} %get-tuple-element.29.refs_0_, s32[40,128]{1,0:T(8,128)S(1)} %get-tuple-element.26.part.refs_1_, s32[40,128]{1,0:T(8,128)S(1)} %collective-permute-done.4.refs_2_), custom_call_target="tpu_custom_call" | custom-call | tf_op jit(solution)/shard_map/pallas_call | solution.py:335
  (2 shorter events, 0.0 us)
Async XLA Ops:
  1.1 1.4 %collective-permute-start = (s32[96,128]{1,0:T(8,128)S(1)}, s32[96,128]{1,0:T(8,128)S(1)}, u32[]{:S(2)}, u32[]{:S(2)}) collective-permute-start(s32[96,128]{1,0:T(8,128)S(1)} %get-tuple-element.21), channel_id=1, source_target_pairs={{0,1},{1,0},{2,3},{3,2},{4,5},{5,4},{6,7},{7,6},{8,9},{9,8},{10,11... | collective-permute-start | bytes 147464 | tf_op jit(solution)/shard_map/ppermute | solution.py:274
  2.5 5.1 %collective-permute-start.1 = (s32[32,128]{1,0:T(8,128)S(1)}, s32[32,128]{1,0:T(8,128)S(1)}, u32[]{:S(2)}, u32[]{:S(2)}) collective-permute-start(s32[32,128]{1,0:T(8,128)S(1)} %get-tuple-element.23), channel_id=1, source_target_pairs={{0,7},{1,6},{2,5},{3,4},{4,3},{5,2},{6,1},{7,0},{8,15},{9,14},{10,... | collective-permute-start | bytes 49160 | tf_op jit(solution)/shard_map/ppermute | solution.py:274
  6.2 3.2 %collective-permute-start.2 = (s32[32,128]{1,0:T(8,128)S(1)}, s32[32,128]{1,0:T(8,128)S(1)}, u32[]{:S(2)}, u32[]{:S(2)}) collective-permute-start(s32[32,128]{1,0:T(8,128)S(1)} %get-tuple-element.24), channel_id=1, source_target_pairs={{0,5},{1,4},{2,7},{3,6},{4,1},{5,0},{6,3},{7,2},{8,13},{9,12},{10,... | collective-permute-start | bytes 49160 | tf_op jit(solution)/shard_map/ppermute | solution.py:274
  6.7 3.2 %collective-permute-start.3 = (s32[32,128]{1,0:T(8,128)S(1)}, s32[32,128]{1,0:T(8,128)S(1)}, u32[]{:S(2)}, u32[]{:S(2)}) collective-permute-start(s32[32,128]{1,0:T(8,128)S(1)} %get-tuple-element.25), channel_id=1, source_target_pairs={{0,3},{1,2},{2,1},{3,0},{4,7},{5,6},{6,5},{7,4},{8,11},{9,10},{10,... | collective-permute-start | bytes 49160 | tf_op jit(solution)/shard_map/ppermute | solution.py:274
  9.8 4.2 %collective-permute-start.4 = (s32[40,128]{1,0:T(8,128)S(1)}, s32[40,128]{1,0:T(8,128)S(1)}, u32[]{:S(2)}, u32[]{:S(2)}) collective-permute-start(s32[40,128]{1,0:T(8,128)S(1)} %get-tuple-element.30), channel_id=1, source_target_pairs={{0,9},{1,8},{2,11},{3,10},{4,13},{5,12},{6,15},{7,14},{8,1},{9,0},... | collective-permute-start | bytes 61448 | tf_op jit(solution)/shard_map/ppermute | solution.py:274

commit v5 on v4

--- a/solution.py
+++ b/solution.py
@@ -10,6 +10,7 @@
 LEVELS = 2
 DIGITS = 2
 LANES = 128
+LOADS = 4
 DEPTH = 64
 
 
@@ -30,15 +31,16 @@
     return destinations(stages[::-1])
 
 
-def answer_kernel(n, polys, assignment, database, queries, key_rows, *refs):
+def answer_kernel(n, polys, assignment, *refs):
+    database, (queries, key_rows), refs = refs[:LOADS], refs[LOADS : LOADS + 2], refs[LOADS + 2 :]
     outs, (rows, key_scratch) = refs[:-2], refs[-2:]
     clients = queries.shape[0]
-    blocks = database.shape[1] // LANES
+    blocks = LOADS * database[0].shape[1] // LANES
     cycle_blocks = blocks // polys
     words = queries[...]
     bytes_ = [jnp.bitwise_and(jnp.right_shift(words, 8 * j), 255) for j in range(4)]
     lhs = jnp.concatenate(bytes_, axis=0).astype(jnp.float32).astype(jnp.bfloat16)
-    rhs = database[...].astype(jnp.float32).astype(jnp.bfloat16)
+    rhs = jnp.concatenate([part[...] for part in database], axis=1).astype(jnp.float32).astype(jnp.bfloat16)
     sums = jnp.dot(lhs, rhs, preferred_element_type=jnp.float32).astype(jnp.int32)
     partial = sums[:clients]
     for j in range(1, 4):
@@ -273,18 +275,21 @@
     def exchange(x, mask):
         return lax.ppermute(x, "col", [(i, i ^ mask) for i in range(n)])
 
+    width = database.shape[1] // LOADS
+    columns = [pl.BlockSpec((database.shape[0], width), lambda _, i=i: (0, i)) for i in range(LOADS)]
     pieces = len(stages[0]) + 1
     rows = n // pieces
     parts = pl.pallas_call(
         functools.partial(answer_kernel, n, polys),
         out_shape=[pltpu.VMEM((rows * (cycle_blocks + chunk), LANES), jnp.int32)] * pieces,
-        in_specs=[smem, vmem, vmem, vmem],
+        grid=(1,),
+        in_specs=[smem, *columns, vmem, vmem],
         out_specs=[vmem] * pieces,
         scratch_shapes=[
             pltpu.VMEM((clients * polys * cycle_blocks, LANES), jnp.int32),
             pltpu.VMEM((max(clients * chunk, 8), LANES), jnp.int32),
         ],
-    )(assignment, database, queries, key_rows)
+    )(assignment, *[database] * LOADS, queries, key_rows)
     mask_poly, digits = pl.pallas_call(
         functools.partial(digit_kernel, polys),
         out_shape=[

time: 15.2 us -> 15.1 us (level)
  no operation moved by 1% of the time
where the time goes in v5:
time: 15.1 us; the launch traced here: 14.9 us
  starting transfers between devices  7.21 us (48%)
  waiting for transfers between devices  4.13 us (27%)
  Pallas kernels  3.52 us (23%)
    ppermute x5, starting transfers between devices, exchange(): return lax.ppermute(x, 'col', [(i, i ^ mask) for i in range(n)])  7.21 us
    ppermute x5, waiting for transfers between devices, exchange(): return lax.ppermute(x, 'col', [(i, i ^ mask) for i in range(n)])  4.13 us
    pallas_call x1, Pallas kernels, on_device(): pl.pallas_call(functools.partial(answer_kernel, n, polys), out_shape=[plt...  1.02 us
    pallas_call x1, Pallas kernels, on_device(): pl.pallas_call(functools.partial(pack_kernel, n, chunk, len(parts)), out_...  0.98 us
    pallas_call x1, Pallas kernels, on_device(): pl.pallas_call(functools.partial(digit_kernel, polys), out_shape=[pltpu.V...  0.92 us
    pallas_call x1, Pallas kernels, on_device(): pl.pallas_call(functools.partial(early_kernel, n, chunk), out_shape=[pltp...  0.58 us
  transfers between devices with their start and end apart: 5, of which 5 were waited for; matrix products, arithmetic and copies ran while one was open for 0% of the time, Pallas kernels for 10%

profile of v5, /device:TPU:0, one launch (start us, length us, event | category | flops | bytes accessed | tf_op | source)
XLA Modules:
  0.0 14.9 jit_solution(1780317506941930793)
XLA Ops:
  0.0 1.0 %shard_map.56 = (s32[96,128]{1,0:T(8,128)S(1)}, s32[96,128]{1,0:T(8,128)S(1)}) custom-call(s32[16]{0:T(128)} %assignment.3, s32[16,2048]{1,0:T(8,128)} %refs_3_.1, s32[16,2048]{1,0:T(8,128)} %refs_3_.1, s32[16,2048]{1,0:T(8,128)} %refs_3_.1, s32[16,2048]{1,0:T(8,128)} %refs_3_.1, s32[8,16]{1,0:T(8,128)} %refs_4_.1, s32[8,512]{1,0:T(8,128)} %refs_5_.1), custom_call_target="tpu_custom_call" | custom-call | tf_op jit(solution)/shard_map/pallas_call | solution.py:282
  1.0 0.5 %collective-permute-start = (s32[96,128]{1,0:T(8,128)S(1)}, s32[96,128]{1,0:T(8,128)S(1)}, u32[]{:S(2)}, u32[]{:S(2)}) collective-permute-start(s32[96,128]{1,0:T(8,128)S(1)} %get-tuple-element.21), channel_id=1, source_target_pairs={{0,1},{1,0},{2,3},{3,2},{4,5},{5,4},{6,7},{7,6},{8,9},{9,8},{10,11... | collective-permute-start | bytes 147464 | tf_op jit(solution)/shard_map/ppermute | solution.py:276
  1.5 0.9 %collective-permute-done.refs_1_ = s32[96,128]{1,0:T(8,128)S(1)} collective-permute-done((s32[96,128]{1,0:T(8,128)S(1)}, s32[96,128]{1,0:T(8,128)S(1)}, u32[]{:S(2)}, u32[]{:S(2)}) %collective-permute-start) | collective-permute-done | bytes 49184 | tf_op jit(solution)/shard_map/ppermute | solution.py:276
  2.4 3.6 %collective-permute-start.1 = (s32[32,128]{1,0:T(8,128)S(1)}, s32[32,128]{1,0:T(8,128)S(1)}, u32[]{:S(2)}, u32[]{:S(2)}) collective-permute-start(s32[32,128]{1,0:T(8,128)S(1)} %get-tuple-element.23), channel_id=1, source_target_pairs={{0,7},{1,6},{2,5},{3,4},{4,3},{5,2},{6,1},{7,0},{8,15},{9,14},{10,... | collective-permute-start | bytes 49160 | tf_op jit(solution)/shard_map/ppermute | solution.py:276
  6.1 0.5 %collective-permute-start.2 = (s32[32,128]{1,0:T(8,128)S(1)}, s32[32,128]{1,0:T(8,128)S(1)}, u32[]{:S(2)}, u32[]{:S(2)}) collective-permute-start(s32[32,128]{1,0:T(8,128)S(1)} %get-tuple-element.24), channel_id=1, source_target_pairs={{0,5},{1,4},{2,7},{3,6},{4,1},{5,0},{6,3},{7,2},{8,13},{9,12},{10,... | collective-permute-start | bytes 49160 | tf_op jit(solution)/shard_map/ppermute | solution.py:276
  6.6 0.2 %collective-permute-start.3 = (s32[32,128]{1,0:T(8,128)S(1)}, s32[32,128]{1,0:T(8,128)S(1)}, u32[]{:S(2)}, u32[]{:S(2)}) collective-permute-start(s32[32,128]{1,0:T(8,128)S(1)} %get-tuple-element.25), channel_id=1, source_target_pairs={{0,3},{1,2},{2,1},{3,0},{4,7},{5,6},{6,5},{7,4},{8,11},{9,10},{10,... | collective-permute-start | bytes 49160 | tf_op jit(solution)/shard_map/ppermute | solution.py:276
  6.7 0.8 %collective-permute-done.1.refs_1_ = s32[32,128]{1,0:T(8,128)S(1)} collective-permute-done((s32[32,128]{1,0:T(8,128)S(1)}, s32[32,128]{1,0:T(8,128)S(1)}, u32[]{:S(2)}, u32[]{:S(2)}) %collective-permute-start.1) | collective-permute-done | bytes 16416 | tf_op jit(solution)/shard_map/ppermute | solution.py:276
  7.5 1.7 %collective-permute-done.2.refs_2_ = s32[32,128]{1,0:T(8,128)S(1)} collective-permute-done((s32[32,128]{1,0:T(8,128)S(1)}, s32[32,128]{1,0:T(8,128)S(1)}, u32[]{:S(2)}, u32[]{:S(2)}) %collective-permute-start.2) | collective-permute-done | bytes 16416 | tf_op jit(solution)/shard_map/ppermute | solution.py:276
  9.2 0.5 %collective-permute-done.3.refs_3_ = s32[32,128]{1,0:T(8,128)S(1)} collective-permute-done((s32[32,128]{1,0:T(8,128)S(1)}, s32[32,128]{1,0:T(8,128)S(1)}, u32[]{:S(2)}, u32[]{:S(2)}) %collective-permute-start.3) | collective-permute-done | bytes 16416 | tf_op jit(solution)/shard_map/ppermute | solution.py:276
  9.7 2.4 %collective-permute-start.4 = (s32[40,128]{1,0:T(8,128)S(1)}, s32[40,128]{1,0:T(8,128)S(1)}, u32[]{:S(2)}, u32[]{:S(2)}) collective-permute-start(s32[40,128]{1,0:T(8,128)S(1)} %get-tuple-element.30), channel_id=1, source_target_pairs={{0,9},{1,8},{2,11},{3,10},{4,13},{5,12},{6,15},{7,14},{8,1},{9,0},... | collective-permute-start | bytes 61448 | tf_op jit(solution)/shard_map/ppermute | solution.py:276
  12.1 0.9 %shard_map.55 = (s32[8,128]{1,0:T(8,128)S(1)}, bf16[256,1024]{1,0:T(8,128)(2,1)S(1)}) custom-call(s32[16]{0:T(128)} %assignment.3, s32[2,1024]{1,0:T(2,128)} %hint.1), custom_call_target="tpu_custom_call" | custom-call | tf_op jit(solution)/shard_map/pallas_call | solution.py:293
  13.0 0.6 %shard_map.59 = (s32[8,128]{1,0:T(8,128)S(1)}, s32[8,128]{1,0:T(8,128)S(1)}, bf16[256,1024]{1,0:T(8,128)(2,1)S(1)}) custom-call(s32[8,128]{1,0:T(8,128)S(1)} %get-tuple-element.18.mask_in, bf16[256,1024]{1,0:T(8,128)(2,1)S(1)} %get-tuple-element.19.digits_in, s32[40,128]{1,0:T(8,128)S(1)} %get-tuple-element.26.part.refs_1_), custom_call_target="tpu_custom_call" | custom-call | tf_op jit(solution)/shard_map/pallas_call | solution.py:307
  13.6 0.3 %collective-permute-done.4.refs_2_ = s32[40,128]{1,0:T(8,128)S(1)} collective-permute-done((s32[40,128]{1,0:T(8,128)S(1)}, s32[40,128]{1,0:T(8,128)S(1)}, u32[]{:S(2)}, u32[]{:S(2)}) %collective-permute-start.4) | collective-permute-done | bytes 20512 | tf_op jit(solution)/shard_map/ppermute | solution.py:276
  13.9 1.0 %shard_map.60 = f32[1,2,1024]{2,1,0:T(2,128)} custom-call(s32[8,128]{1,0:T(8,128)S(1)} %get-tuple-element.27.mask_in, bf16[256,1024]{1,0:T(8,128)(2,1)S(1)} %get-tuple-element.28.digits, s32[8,128]{1,0:T(8,128)S(1)} %get-tuple-element.29.refs_0_, s32[40,128]{1,0:T(8,128)S(1)} %get-tuple-element.26.part.refs_1_, s32[40,128]{1,0:T(8,128)S(1)} %collective-permute-done.4.refs_2_), custom_call_target="tpu_custom_call" | custom-call | tf_op jit(solution)/shard_map/pallas_call | solution.py:340
  (2 shorter events, 0.0 us)
Async XLA Ops:
  1.0 1.4 %collective-permute-start = (s32[96,128]{1,0:T(8,128)S(1)}, s32[96,128]{1,0:T(8,128)S(1)}, u32[]{:S(2)}, u32[]{:S(2)}) collective-permute-start(s32[96,128]{1,0:T(8,128)S(1)} %get-tuple-element.21), channel_id=1, source_target_pairs={{0,1},{1,0},{2,3},{3,2},{4,5},{5,4},{6,7},{7,6},{8,9},{9,8},{10,11... | collective-permute-start | bytes 147464 | tf_op jit(solution)/shard_map/ppermute | solution.py:276
  2.4 5.1 %collective-permute-start.1 = (s32[32,128]{1,0:T(8,128)S(1)}, s32[32,128]{1,0:T(8,128)S(1)}, u32[]{:S(2)}, u32[]{:S(2)}) collective-permute-start(s32[32,128]{1,0:T(8,128)S(1)} %get-tuple-element.23), channel_id=1, source_target_pairs={{0,7},{1,6},{2,5},{3,4},{4,3},{5,2},{6,1},{7,0},{8,15},{9,14},{10,... | collective-permute-start | bytes 49160 | tf_op jit(solution)/shard_map/ppermute | solution.py:276
  6.1 3.2 %collective-permute-start.2 = (s32[32,128]{1,0:T(8,128)S(1)}, s32[32,128]{1,0:T(8,128)S(1)}, u32[]{:S(2)}, u32[]{:S(2)}) collective-permute-start(s32[32,128]{1,0:T(8,128)S(1)} %get-tuple-element.24), channel_id=1, source_target_pairs={{0,5},{1,4},{2,7},{3,6},{4,1},{5,0},{6,3},{7,2},{8,13},{9,12},{10,... | collective-permute-start | bytes 49160 | tf_op jit(solution)/shard_map/ppermute | solution.py:276
  6.6 3.2 %collective-permute-start.3 = (s32[32,128]{1,0:T(8,128)S(1)}, s32[32,128]{1,0:T(8,128)S(1)}, u32[]{:S(2)}, u32[]{:S(2)}) collective-permute-start(s32[32,128]{1,0:T(8,128)S(1)} %get-tuple-element.25), channel_id=1, source_target_pairs={{0,3},{1,2},{2,1},{3,0},{4,7},{5,6},{6,5},{7,4},{8,11},{9,10},{10,... | collective-permute-start | bytes 49160 | tf_op jit(solution)/shard_map/ppermute | solution.py:276
  9.7 4.2 %collective-permute-start.4 = (s32[40,128]{1,0:T(8,128)S(1)}, s32[40,128]{1,0:T(8,128)S(1)}, u32[]{:S(2)}, u32[]{:S(2)}) collective-permute-start(s32[40,128]{1,0:T(8,128)S(1)} %get-tuple-element.30), channel_id=1, source_target_pairs={{0,9},{1,8},{2,11},{3,10},{4,13},{5,12},{6,15},{7,14},{8,1},{9,0},... | collective-permute-start | bytes 61448 | tf_op jit(solution)/shard_map/ppermute | solution.py:276

commit v6 on v5

--- a/solution.py
+++ b/solution.py
@@ -16,19 +16,40 @@
 
 def stages_of(n):
     bits = [1 << k for k in range(n.bit_length() - 1)]
-    pair = [bits[1] | bits[2] | 1, bits[2] | 1, bits[1] | 1] if len(bits) > 2 else [b | 1 for b in bits[1:2]]
-    return [[1]] + [pair] * (len(pair) > 0) + [[b | 1] for b in bits[3:]]
-
-
-def destinations(stages):
-    rows = [0]
+    pair = [(3, 1), (7, 1), (5, 0)] if len(bits) > 2 else [(b | 1, 0) for b in bits[1:2]]
+    return [[(1, 0)]] + [pair] * (len(pair) > 0) + [[(b | 1, 0)] for b in bits[3:]]
+
+
+def moved(move, i):
+    mask, twist = move
+    if twist:
+        return i ^ mask ^ ((i & 2) << 1)
+    return i ^ mask
+
+
+def back(move):
+    mask, twist = move
+    return (mask ^ (mask & 2) << 1 if twist else mask, twist)
+
+
+def follow(steps, i):
+    for move in steps:
+        i = moved(move, i)
+    return i
+
+
+def destinations(stages, me):
+    rows = [[]]
     for stage in reversed(stages):
-        rows = [r ^ mask for mask in [0] + stage for r in rows]
-    return rows
-
-
-def sources(stages):
-    return destinations(stages[::-1])
+        rows = rows + [[move] + row for move in stage for row in rows]
+    return [follow(row, me) for row in rows]
+
+
+def sources(stages, me):
+    blocks = [[]]
+    for stage in stages:
+        blocks = blocks + [[back(move)] + block for move in stage for block in blocks]
+    return [follow(block, me) for block in blocks]
 
 
 def answer_kernel(n, polys, assignment, *refs):
@@ -52,8 +73,8 @@
     for m in range(chunk):
         key_scratch[pl.ds(m, clients, stride=chunk), :] = key_rows[:, m * LANES : (m + 1) * LANES]
     me = lax.axis_index("col")
-    for r, mask in enumerate(destinations(stages_of(n))):
-        unit = assignment[jnp.bitwise_xor(me, mask)]
+    for r, owner in enumerate(destinations(stages_of(n), me)):
+        unit = assignment[owner]
         out, place = outs[r // share], r % share
         out[place * cycle_blocks : (place + 1) * cycle_blocks, :] = rows[
             pl.ds(pl.multiple_of(unit * cycle_blocks, cycle_blocks), cycle_blocks), :
@@ -144,8 +165,8 @@
     return jnp.concatenate(rows, axis=0).astype(jnp.float32).astype(jnp.bfloat16)
 
 
-def switch(keys, digits, blocks):
-    sums = jnp.dot(key_matrix(keys), digits, preferred_element_type=jnp.float32).astype(jnp.int32)
+def switch(matrix, digits, blocks):
+    sums = jnp.dot(matrix, digits, preferred_element_type=jnp.float32).astype(jnp.int32)
     lane = lax.broadcasted_iota(jnp.int32, (blocks, LANES), 1)
     results = []
     for p in range(2):
@@ -175,33 +196,34 @@
     digits_out[...] = toeplitz(automorph(mask, 0))
 
 
-def holds_first(n, stages):
-    return jnp.logical_and(lax.axis_index("col") < n // 2, stages[-1] == [n // 2 + 1])
-
-
-def key_table(keys, level, cycle_blocks):
-    return [
+def halves_by_level(n, stages):
+    return LEVELS == 2 and stages[-1] == [(n // 2 + 1, 0)]
+
+
+def level_matrix(keys, level, cycle_blocks):
+    table = [
         [keys[pl.ds(((level * DIGITS + t) * 2 + p) * cycle_blocks, cycle_blocks), :] for p in range(2)]
         for t in range(DIGITS)
     ]
-
-
-def place_keys(n, chunk, cycle_blocks, away, part, keys):
-    me = lax.axis_index("col")
-    for slot, distance in enumerate(away):
+    return key_matrix(table)
+
+
+def place_keys(total, chunk, cycle_blocks, origins, part, keys):
+    for slot, origin in enumerate(origins):
         first = cycle_blocks + slot * chunk
-        keys[pl.ds(jnp.bitwise_xor(me, distance) * chunk, chunk), :] = part[first : first + chunk, :]
-
-
-def early_kernel(n, chunk, mask_in, digits_in, part, mask_out, change_out, digits_out, keys):
-    stages = stages_of(n)
-    early = holds_first(n, stages)
+        keys[pl.ds((origin & (total - 1)) * chunk, chunk), :] = part[first : first + chunk, :]
+
+
+def early_kernel(n, chunk, mask_in, digits_in, part, mask_out, change_out, digits_out, matrix_out, keys):
     cycle_blocks = mask_in.shape[0]
+    place_keys(n // 2, chunk, cycle_blocks, sources(stages_of(n)[:-1], lax.axis_index("col")), part, keys)
+    matrix = level_matrix(keys, 0, cycle_blocks)
+    matrix_out[...] = matrix
+    early = lax.axis_index("col") < n // 2
 
     @pl.when(early)
     def _():
-        place_keys(n, chunk, cycle_blocks, sources(stages[:-1]), part, keys)
-        change = switch(key_table(keys, 0, cycle_blocks), digits_in[...], cycle_blocks)
+        change = switch(matrix, digits_in[...], cycle_blocks)
         mask = mask_in[...] + change[0]
         mask_out[...] = mask
         change_out[...] = change[1]
@@ -214,47 +236,59 @@
         digits_out[...] = digits_in[...]
 
 
+def finish(level, mask, value, digits, matrices, packed):
+    cycle_blocks = mask.shape[0]
+    for i, matrix in enumerate(matrices):
+        current = digits[...] if i == 0 else toeplitz(automorph(mask, level))
+        change = switch(matrix(), current, cycle_blocks)
+        mask = mask + change[0]
+        value = value + automorph(value, level) + change[1]
+        level += 1
+    for p, words in enumerate((mask, value)):
+        scaled = words.astype(jnp.float32) * 2.0**-32
+        for b in range(cycle_blocks):
+            packed[0, p : p + 1, b * LANES : (b + 1) * LANES] = scaled[b : b + 1, :]
+
+
+def sum_answers(parts, cycle_blocks):
+    value = parts[0][:cycle_blocks, :]
+    for part in parts[1:]:
+        value = value + part[:cycle_blocks, :]
+    return value
+
+
+def late_kernel(n, chunk, mask_in, digits, change_in, own_matrix, own, got, packed, keys):
+    cycle_blocks = mask_in.shape[0]
+    origins = sources(stages_of(n), lax.axis_index("col"))
+    early = lax.axis_index("col") < n // 2
+
+    def received():
+        place_keys(n // 2, chunk, cycle_blocks, origins[n // 2 :], got, keys)
+        return level_matrix(keys, 0, cycle_blocks)
+
+    @pl.when(early)
+    def _():
+        value = sum_answers((own, got), cycle_blocks)
+        finish(1, mask_in[...], value + automorph(value, 0) + change_in[...], digits, [received], packed)
+
+    @pl.when(jnp.logical_not(early))
+    def _():
+        value = sum_answers((own, got), cycle_blocks)
+        finish(0, mask_in[...], value, digits, [received, lambda: own_matrix[...]], packed)
+
+
 def pack_kernel(n, chunk, partners, mask_in, digits, *refs):
     cycle_blocks = mask_in.shape[0]
-    stages = stages_of(n)
     if chunk:
-        change_in, *parts, packed, keys = refs
+        *parts, packed, keys = refs
         stacked = n // partners
-        away = sources(stages)
+        away = sources(stages_of(n), lax.axis_index("col"))
         for i, part in enumerate(parts):
             place_keys(n, chunk, cycle_blocks, away[i * stacked : (i + 1) * stacked], part, keys)
     else:
         *parts, keys, packed = refs
-
-    def finish(level, mask, value):
-        current = digits[...]
-        while level < LEVELS:
-            change = switch(key_table(keys, level, cycle_blocks), current, cycle_blocks)
-            mask = mask + change[0]
-            value = value + automorph(value, level) + change[1]
-            level += 1
-            if level < LEVELS:
-                current = toeplitz(automorph(mask, level))
-        for p, words in enumerate((mask, value)):
-            scaled = words.astype(jnp.float32) * 2.0**-32
-            for b in range(cycle_blocks):
-                packed[0, p : p + 1, b * LANES : (b + 1) * LANES] = scaled[b : b + 1, :]
-
-    value = parts[0][:cycle_blocks, :]
-    for part in parts[1:]:
-        value = value + part[:cycle_blocks, :]
-    if not chunk:
-        finish(0, mask_in[...], value)
-        return
-    early = holds_first(n, stages)
-
-    @pl.when(early)
-    def _():
-        finish(1, mask_in[...], value + automorph(value, 0) + change_in[...])
-
-    @pl.when(jnp.logical_not(early))
-    def _():
-        finish(0, mask_in[...], value)
+    matrices = [functools.partial(level_matrix, keys, level, cycle_blocks) for level in range(LEVELS)]
+    finish(0, mask_in[...], sum_answers(parts, cycle_blocks), digits, matrices, packed)
 
 
 def near(x):
@@ -272,8 +306,8 @@
     smem = pl.BlockSpec(memory_space=pltpu.SMEM)
     chunk = key_width // LANES if key_width % LANES == 0 else 0
 
-    def exchange(x, mask):
-        return lax.ppermute(x, "col", [(i, i ^ mask) for i in range(n)])
+    def exchange(x, move):
+        return lax.ppermute(x, "col", [(i, moved(move, i)) for i in range(n)])
 
     width = database.shape[1] // LOADS
     columns = [pl.BlockSpec((database.shape[0], width), lambda _, i=i: (0, i)) for i in range(LOADS)]
@@ -302,17 +336,20 @@
 
     stacked = 1
     extra = []
+    halves = chunk and halves_by_level(n, stages)
     for step, stage in enumerate(stages):
-        if chunk and step == len(stages) - 1:
-            mask_poly, change, digits = pl.pallas_call(
+        if halves and step == len(stages) - 1:
+            matrix = (2 * 4 * 2 * cycle_blocks, 2 * DIGITS * DEPTH)
+            mask_poly, change, digits, own_matrix = pl.pallas_call(
                 functools.partial(early_kernel, n, chunk),
-                out_shape=[pltpu.VMEM(mask_poly.shape, jnp.int32)] * 2 + [pltpu.VMEM(digits.shape, jnp.bfloat16)],
+                out_shape=[pltpu.VMEM(mask_poly.shape, jnp.int32)] * 2
+                + [pltpu.VMEM(digits.shape, jnp.bfloat16), pltpu.VMEM(matrix, jnp.bfloat16)],
                 in_specs=[vmem] * 3,
-                out_specs=[vmem] * 3,
-                scratch_shapes=[pltpu.VMEM((n * chunk, LANES), jnp.int32)],
+                out_specs=[vmem] * 4,
+                scratch_shapes=[pltpu.VMEM((n // 2 * chunk, LANES), jnp.int32)],
             )(near(mask_poly), near(digits), near(parts[0]))
-            extra = [change]
-        parts = [parts[0]] + [exchange(part, mask) for part, mask in zip(parts[1:], stage)]
+            extra = [change, own_matrix]
+        parts = [parts[0]] + [exchange(part, move) for part, move in zip(parts[1:], stage)]
         stacked *= len(parts)
         if step < len(stages) - 1:
             pieces = len(stages[step + 1]) + 1
@@ -328,17 +365,15 @@
     operands = [near(x) for x in (mask_poly, digits, *extra, *parts)]
     if not chunk:
         me = lax.axis_index("col")
-        order = jnp.bitwise_xor(jnp.array(destinations(stages), jnp.int32), me)
-        keys = jnp.take(key_rows, assignment[order] // polys, axis=0)[None]
+        owners = assignment[jnp.stack(destinations(stages, me))] // polys
+        keys = jnp.take(key_rows, owners, axis=0)[None]
         for stage in stages:
             cuts = jnp.split(keys, len(stage) + 1, axis=1)
-            keys = jnp.concatenate([cuts[0]] + [exchange(x, mask) for x, mask in zip(cuts[1:], stage)], axis=0)
-        away = sources(stages)
-        places = jnp.array([away.index(i) for i in range(n)], jnp.int32)
-        places = places[jnp.bitwise_xor(jnp.arange(n, dtype=jnp.int32), me)]
+            keys = jnp.concatenate([cuts[0]] + [exchange(x, move) for x, move in zip(cuts[1:], stage)], axis=0)
+        places = jnp.zeros((n,), jnp.int32).at[jnp.stack(sources(stages, me))].set(jnp.arange(n, dtype=jnp.int32))
         operands.append(jnp.take(keys.reshape(n, key_width), places, axis=0).reshape(-1, LANES))
     return pl.pallas_call(
-        functools.partial(pack_kernel, n, chunk, len(parts)),
+        functools.partial(late_kernel, n, chunk) if halves else functools.partial(pack_kernel, n, chunk, len(parts)),
         out_shape=jax.ShapeDtypeStruct((1, 2, cycle_width), jnp.float32),
         in_specs=[vmem] * len(operands),
         out_specs=vmem,

time: 15.1 us -> 14.9 us (0.987)
  waiting for transfers between devices: 4.13 us -> 2.48 us
  starting transfers between devices: 7.21 us -> 8.59 us
    ppermute x5, waiting for transfers between devices: 4.13 us -> 2.48 us  [exchange(): return lax.ppermute(x, 'col', [(i, moved(move, i)) for i in range(n)])]
    ppermute x5, starting transfers between devices: 7.21 us -> 8.59 us  [exchange(): return lax.ppermute(x, 'col', [(i, moved(move, i)) for i in range(n)])]
  transfers between devices with their start and end apart: 5 -> 5, of which waited for: 5 -> 3; matrix products, arithmetic and copies ran while one was open for 0% -> 0% of each run, Pallas kernels for 10% -> 11%
where the time goes in v6:
time: 14.9 us; the launch traced here: 14.7 us
  starting transfers between devices  8.59 us (58%)
  Pallas kernels  3.57 us (24%)
  waiting for transfers between devices  2.48 us (17%)
    ppermute x5, starting transfers between devices, exchange(): return lax.ppermute(x, 'col', [(i, moved(move, i)) for i in range(n)])  8.59 us
    ppermute x5, waiting for transfers between devices, exchange(): return lax.ppermute(x, 'col', [(i, moved(move, i)) for i in range(n)])  2.48 us
    pallas_call x1, Pallas kernels, on_device(): pl.pallas_call(functools.partial(answer_kernel, n, polys), out_shape=[plt...  1.02 us
    pallas_call x1, Pallas kernels, on_device(): pl.pallas_call(functools.partial(late_kernel, n, chunk) if halves else fu...  0.99 us
    pallas_call x1, Pallas kernels, on_device(): pl.pallas_call(functools.partial(digit_kernel, polys), out_shape=[pltpu.V...  0.92 us
    pallas_call x1, Pallas kernels, on_device(): pl.pallas_call(functools.partial(early_kernel, n, chunk), out_shape=[pltp...  0.62 us
  transfers between devices with their start and end apart: 5, of which 3 were waited for; matrix products, arithmetic and copies ran while one was open for 0% of the time, Pallas kernels for 11%

profile of v6, /device:TPU:0, one launch (start us, length us, event | category | flops | bytes accessed | tf_op | source)
XLA Modules:
  0.0 14.7 jit_solution(9624221992149774307)
XLA Ops:
  0.0 1.0 %shard_map.56 = (s32[96,128]{1,0:T(8,128)S(1)}, s32[96,128]{1,0:T(8,128)S(1)}) custom-call(s32[16]{0:T(128)} %assignment.3, s32[16,2048]{1,0:T(8,128)} %refs_3_.1, s32[16,2048]{1,0:T(8,128)} %refs_3_.1, s32[16,2048]{1,0:T(8,128)} %refs_3_.1, s32[16,2048]{1,0:T(8,128)} %refs_3_.1, s32[8,16]{1,0:T(8,128)} %refs_4_.1, s32[8,512]{1,0:T(8,128)} %refs_5_.1), custom_call_target="tpu_custom_call" | custom-call | tf_op jit(solution)/shard_map/pallas_call | solution.py:316
  1.0 0.5 %collective-permute-start = (s32[96,128]{1,0:T(8,128)S(1)}, s32[96,128]{1,0:T(8,128)S(1)}, u32[]{:S(2)}, u32[]{:S(2)}) collective-permute-start(s32[96,128]{1,0:T(8,128)S(1)} %get-tuple-element.22), channel_id=1, source_target_pairs={{0,1},{1,0},{2,3},{3,2},{4,5},{5,4},{6,7},{7,6},{8,9},{9,8},{10,11... | collective-permute-start | bytes 147464 | tf_op jit(solution)/shard_map/ppermute | solution.py:310
  1.5 0.9 %collective-permute-done.refs_1_ = s32[96,128]{1,0:T(8,128)S(1)} collective-permute-done((s32[96,128]{1,0:T(8,128)S(1)}, s32[96,128]{1,0:T(8,128)S(1)}, u32[]{:S(2)}, u32[]{:S(2)}) %collective-permute-start) | collective-permute-done | bytes 49184 | tf_op jit(solution)/shard_map/ppermute | solution.py:310
  2.4 2.6 %collective-permute-start.1 = (s32[32,128]{1,0:T(8,128)S(1)}, s32[32,128]{1,0:T(8,128)S(1)}, u32[]{:S(2)}, u32[]{:S(2)}) collective-permute-start(s32[32,128]{1,0:T(8,128)S(1)} %get-tuple-element.24), channel_id=1, source_target_pairs={{0,3},{1,2},{2,5},{3,4},{4,7},{5,6},{6,1},{7,0},{8,11},{9,10},{10,... | collective-permute-start | bytes 49160 | tf_op jit(solution)/shard_map/ppermute | solution.py:310
  5.1 1.1 %collective-permute-start.2 = (s32[32,128]{1,0:T(8,128)S(1)}, s32[32,128]{1,0:T(8,128)S(1)}, u32[]{:S(2)}, u32[]{:S(2)}) collective-permute-start(s32[32,128]{1,0:T(8,128)S(1)} %get-tuple-element.25), channel_id=1, source_target_pairs={{0,7},{1,6},{2,1},{3,0},{4,3},{5,2},{6,5},{7,4},{8,15},{9,14},{10,... | collective-permute-start | bytes 49160 | tf_op jit(solution)/shard_map/ppermute | solution.py:310
  6.1 1.6 %collective-permute-start.3 = (s32[32,128]{1,0:T(8,128)S(1)}, s32[32,128]{1,0:T(8,128)S(1)}, u32[]{:S(2)}, u32[]{:S(2)}) collective-permute-start(s32[32,128]{1,0:T(8,128)S(1)} %get-tuple-element.26), channel_id=1, source_target_pairs={{0,5},{1,4},{2,7},{3,6},{4,1},{5,0},{6,3},{7,2},{8,13},{9,12},{10,... | collective-permute-start | bytes 49160 | tf_op jit(solution)/shard_map/ppermute | solution.py:310
  7.8 0.0 collective-permute-done.1.refs_1_
  7.8 0.5 %collective-permute-done.2.refs_2_ = s32[32,128]{1,0:T(8,128)S(1)} collective-permute-done((s32[32,128]{1,0:T(8,128)S(1)}, s32[32,128]{1,0:T(8,128)S(1)}, u32[]{:S(2)}, u32[]{:S(2)}) %collective-permute-start.2) | collective-permute-done | bytes 16416 | tf_op jit(solution)/shard_map/ppermute | solution.py:310
  8.3 1.1 %collective-permute-done.3.refs_3_ = s32[32,128]{1,0:T(8,128)S(1)} collective-permute-done((s32[32,128]{1,0:T(8,128)S(1)}, s32[32,128]{1,0:T(8,128)S(1)}, u32[]{:S(2)}, u32[]{:S(2)}) %collective-permute-start.3) | collective-permute-done | bytes 16416 | tf_op jit(solution)/shard_map/ppermute | solution.py:310
  9.4 2.7 %collective-permute-start.4 = (s32[40,128]{1,0:T(8,128)S(1)}, s32[40,128]{1,0:T(8,128)S(1)}, u32[]{:S(2)}, u32[]{:S(2)}) collective-permute-start(s32[40,128]{1,0:T(8,128)S(1)} %get-tuple-element.32), channel_id=1, source_target_pairs={{0,9},{1,8},{2,11},{3,10},{4,13},{5,12},{6,15},{7,14},{8,1},{9,0},... | collective-permute-start | bytes 61448 | tf_op jit(solution)/shard_map/ppermute | solution.py:310
  12.1 0.9 %shard_map.55 = (s32[8,128]{1,0:T(8,128)S(1)}, bf16[256,1024]{1,0:T(8,128)(2,1)S(1)}) custom-call(s32[16]{0:T(128)} %assignment.3, s32[2,1024]{1,0:T(2,128)} %hint.1), custom_call_target="tpu_custom_call" | custom-call | tf_op jit(solution)/shard_map/pallas_call | solution.py:327
  13.0 0.6 %shard_map.59 = (s32[8,128]{1,0:T(8,128)S(1)}, s32[8,128]{1,0:T(8,128)S(1)}, bf16[256,1024]{1,0:T(8,128)(2,1)S(1)}, bf16[128,256]{1,0:T(8,128)(2,1)S(1)}) custom-call(s32[8,128]{1,0:T(8,128)S(1)} %get-tuple-element.19.mask_in, bf16[256,1024]{1,0:T(8,128)(2,1)S(1)} %get-tuple-element.20.digits_in, s32[40,128]{1,0:T(8,128)S(1)} %get-tuple-element.27.part.own), custom_call_target="tpu_custom_call" | custom-call | tf_op jit(solution)/shard_map/pallas_call | solution.py:343
  13.7 0.0 collective-permute-done.4.got
  13.7 1.0 %shard_map.60 = f32[1,2,1024]{2,1,0:T(2,128)} custom-call(s32[8,128]{1,0:T(8,128)S(1)} %get-tuple-element.28.mask_in, bf16[256,1024]{1,0:T(8,128)(2,1)S(1)} %get-tuple-element.29.digits, s32[8,128]{1,0:T(8,128)S(1)} %get-tuple-element.30.change_in, bf16[128,256]{1,0:T(8,128)(2,1)S(1)} %get-tuple-element.31.own_matrix, ...), custom_call_target="tpu_custom_call" | custom-call | tf_op jit(solution)/shard_map/pallas_call | solution.py:375
  (2 shorter events, 0.0 us)
Async XLA Ops:
  1.0 1.4 %collective-permute-start = (s32[96,128]{1,0:T(8,128)S(1)}, s32[96,128]{1,0:T(8,128)S(1)}, u32[]{:S(2)}, u32[]{:S(2)}) collective-permute-start(s32[96,128]{1,0:T(8,128)S(1)} %get-tuple-element.22), channel_id=1, source_target_pairs={{0,1},{1,0},{2,3},{3,2},{4,5},{5,4},{6,7},{7,6},{8,9},{9,8},{10,11... | collective-permute-start | bytes 147464 | tf_op jit(solution)/shard_map/ppermute | solution.py:310
  2.4 5.3 %collective-permute-start.1 = (s32[32,128]{1,0:T(8,128)S(1)}, s32[32,128]{1,0:T(8,128)S(1)}, u32[]{:S(2)}, u32[]{:S(2)}) collective-permute-start(s32[32,128]{1,0:T(8,128)S(1)} %get-tuple-element.24), channel_id=1, source_target_pairs={{0,3},{1,2},{2,5},{3,4},{4,7},{5,6},{6,1},{7,0},{8,11},{9,10},{10,... | collective-permute-start | bytes 49160 | tf_op jit(solution)/shard_map/ppermute | solution.py:310
  5.1 3.2 %collective-permute-start.2 = (s32[32,128]{1,0:T(8,128)S(1)}, s32[32,128]{1,0:T(8,128)S(1)}, u32[]{:S(2)}, u32[]{:S(2)}) collective-permute-start(s32[32,128]{1,0:T(8,128)S(1)} %get-tuple-element.25), channel_id=1, source_target_pairs={{0,7},{1,6},{2,1},{3,0},{4,3},{5,2},{6,5},{7,4},{8,15},{9,14},{10,... | collective-permute-start | bytes 49160 | tf_op jit(solution)/shard_map/ppermute | solution.py:310
  6.1 3.2 %collective-permute-start.3 = (s32[32,128]{1,0:T(8,128)S(1)}, s32[32,128]{1,0:T(8,128)S(1)}, u32[]{:S(2)}, u32[]{:S(2)}) collective-permute-start(s32[32,128]{1,0:T(8,128)S(1)} %get-tuple-element.26), channel_id=1, source_target_pairs={{0,5},{1,4},{2,7},{3,6},{4,1},{5,0},{6,3},{7,2},{8,13},{9,12},{10,... | collective-permute-start | bytes 49160 | tf_op jit(solution)/shard_map/ppermute | solution.py:310
  9.4 4.3 %collective-permute-start.4 = (s32[40,128]{1,0:T(8,128)S(1)}, s32[40,128]{1,0:T(8,128)S(1)}, u32[]{:S(2)}, u32[]{:S(2)}) collective-permute-start(s32[40,128]{1,0:T(8,128)S(1)} %get-tuple-element.32), channel_id=1, source_target_pairs={{0,9},{1,8},{2,11},{3,10},{4,13},{5,12},{6,15},{7,14},{8,1},{9,0},... | collective-permute-start | bytes 61448 | tf_op jit(solution)/shard_map/ppermute | solution.py:310

commit v7 on v6

--- a/solution.py
+++ b/solution.py
@@ -84,7 +84,8 @@
             out[first : first + chunk, :] = key_scratch[pl.ds(unit // polys * chunk, chunk), :]
 
 
-def join_kernel(cycle_blocks, rows, chunk, partners, *refs):
+def join_kernel(cycle_blocks, rows, chunk, partners, after, *refs):
+    del after
     parts, outs = refs[:partners], refs[partners:]
     share = rows // len(outs)
     cut = rows * cycle_blocks
@@ -187,7 +188,8 @@
     return results
 
 
-def digit_kernel(polys, assignment, hint, mask_out, digits_out):
+def digit_kernel(polys, assignment, hint, after, mask_out, digits_out):
+    del after
     cycle_blocks = mask_out.shape[0]
     poly = assignment[lax.axis_index("col")] % polys
     row = hint[pl.ds(poly, 1), :]
@@ -304,6 +306,7 @@
     stages = stages_of(n)
     vmem = pl.BlockSpec(memory_space=pltpu.VMEM)
     smem = pl.BlockSpec(memory_space=pltpu.SMEM)
+    anywhere = pl.BlockSpec(memory_space=pl.ANY)
     chunk = key_width // LANES if key_width % LANES == 0 else 0
 
     def exchange(x, move):
@@ -324,20 +327,24 @@
             pltpu.VMEM((max(clients * chunk, 8), LANES), jnp.int32),
         ],
     )(assignment, *[database] * LOADS, queries, key_rows)
-    mask_poly, digits = pl.pallas_call(
-        functools.partial(digit_kernel, polys),
-        out_shape=[
-            pltpu.VMEM((cycle_blocks, LANES), jnp.int32),
-            pltpu.VMEM((2 * DIGITS * DEPTH, cycle_width), jnp.bfloat16),
-        ],
-        in_specs=[smem, vmem],
-        out_specs=[vmem] * 2,
-    )(assignment, hint)
+    def digits_after(after):
+        return pl.pallas_call(
+            functools.partial(digit_kernel, polys),
+            out_shape=[
+                pltpu.VMEM((cycle_blocks, LANES), jnp.int32),
+                pltpu.VMEM((2 * DIGITS * DEPTH, cycle_width), jnp.bfloat16),
+            ],
+            in_specs=[smem, vmem, anywhere],
+            out_specs=[vmem] * 2,
+        )(assignment, hint, after)
 
     stacked = 1
     extra = []
     halves = chunk and halves_by_level(n, stages)
+    before_last = max(len(stages) - 2, 0)
     for step, stage in enumerate(stages):
+        if step == before_last:
+            mask_poly, digits = digits_after(near(parts[0]))
         if halves and step == len(stages) - 1:
             matrix = (2 * 4 * 2 * cycle_blocks, 2 * DIGITS * DEPTH)
             mask_poly, change, digits, own_matrix = pl.pallas_call(
@@ -357,9 +364,9 @@
             parts = pl.pallas_call(
                 functools.partial(join_kernel, cycle_blocks, rows, chunk, len(parts)),
                 out_shape=[pltpu.VMEM((share * (cycle_blocks + stacked * chunk), LANES), jnp.int32)] * pieces,
-                in_specs=[vmem] * len(parts),
+                in_specs=[anywhere] + [vmem] * len(parts),
                 out_specs=[vmem] * pieces,
-            )(*map(near, parts))
+            )(near(mask_poly) if step == before_last else assignment, *map(near, parts))
             rows = share
 
     operands = [near(x) for x in (mask_poly, digits, *extra, *parts)]

time: 14.9 us -> 14.8 us (level)
  transfers between devices with their start and end apart: 5 -> 5, of which waited for: 3 -> 3; matrix products, arithmetic and copies ran while one was open for 0% -> 0% of each run, Pallas kernels for 11% -> 10%
where the time goes in v7:
time: 14.8 us; the launch traced here: 14.6 us
  starting transfers between devices  8.59 us (58%)
  Pallas kernels  3.55 us (24%)
  waiting for transfers between devices  2.39 us (16%)
    ppermute x5, starting transfers between devices, exchange(): return lax.ppermute(x, 'col', [(i, moved(move, i)) for i in range(n)])  8.59 us
    ppermute x5, waiting for transfers between devices, exchange(): return lax.ppermute(x, 'col', [(i, moved(move, i)) for i in range(n)])  2.39 us
    pallas_call x1, Pallas kernels, on_device(): pl.pallas_call(functools.partial(answer_kernel, n, polys), out_shape=[plt...  1.02 us
    pallas_call x1, Pallas kernels, on_device(): pl.pallas_call(functools.partial(late_kernel, n, chunk) if halves else fu...  0.98 us
    pallas_call x1, Pallas kernels, digits_after(): pl.pallas_call(functools.partial(digit_kernel, polys), out_shape=[pltpu.V...  0.93 us
    pallas_call x1, Pallas kernels, on_device(): pl.pallas_call(functools.partial(early_kernel, n, chunk), out_shape=[pltp...  0.61 us
  transfers between devices with their start and end apart: 5, of which 3 were waited for; matrix products, arithmetic and copies ran while one was open for 0% of the time, Pallas kernels for 10%

profile of v7, /device:TPU:0, one launch (start us, length us, event | category | flops | bytes accessed | tf_op | source)
XLA Modules:
  0.0 14.6 jit_solution(3562977222658732959)
XLA Ops:
  0.0 1.0 %shard_map.55 = (s32[96,128]{1,0:T(8,128)S(1)}, s32[96,128]{1,0:T(8,128)S(1)}) custom-call(s32[16]{0:T(128)} %assignment.3, s32[16,2048]{1,0:T(8,128)} %refs_3_.1, s32[16,2048]{1,0:T(8,128)} %refs_3_.1, s32[16,2048]{1,0:T(8,128)} %refs_3_.1, s32[16,2048]{1,0:T(8,128)} %refs_3_.1, s32[8,16]{1,0:T(8,128)} %refs_4_.1, s32[8,512]{1,0:T(8,128)} %refs_5_.1), custom_call_target="tpu_custom_call" | custom-call | tf_op jit(solution)/shard_map/pallas_call | solution.py:319
  1.0 0.5 %collective-permute-start = (s32[96,128]{1,0:T(8,128)S(1)}, s32[96,128]{1,0:T(8,128)S(1)}, u32[]{:S(2)}, u32[]{:S(2)}) collective-permute-start(s32[96,128]{1,0:T(8,128)S(1)} %get-tuple-element.20), channel_id=1, source_target_pairs={{0,1},{1,0},{2,3},{3,2},{4,5},{5,4},{6,7},{7,6},{8,9},{9,8},{10,11... | collective-permute-start | bytes 147464 | tf_op jit(solution)/shard_map/ppermute | solution.py:313
  1.5 0.9 %collective-permute-done.refs_1_ = s32[96,128]{1,0:T(8,128)S(1)} collective-permute-done((s32[96,128]{1,0:T(8,128)S(1)}, s32[96,128]{1,0:T(8,128)S(1)}, u32[]{:S(2)}, u32[]{:S(2)}) %collective-permute-start) | collective-permute-done | bytes 49184 | tf_op jit(solution)/shard_map/ppermute | solution.py:313
  2.4 2.6 %collective-permute-start.1 = (s32[32,128]{1,0:T(8,128)S(1)}, s32[32,128]{1,0:T(8,128)S(1)}, u32[]{:S(2)}, u32[]{:S(2)}) collective-permute-start(s32[32,128]{1,0:T(8,128)S(1)} %get-tuple-element.24), channel_id=1, source_target_pairs={{0,3},{1,2},{2,5},{3,4},{4,7},{5,6},{6,1},{7,0},{8,11},{9,10},{10,... | collective-permute-start | bytes 49160 | tf_op jit(solution)/shard_map/ppermute | solution.py:313
  5.1 1.1 %collective-permute-start.2 = (s32[32,128]{1,0:T(8,128)S(1)}, s32[32,128]{1,0:T(8,128)S(1)}, u32[]{:S(2)}, u32[]{:S(2)}) collective-permute-start(s32[32,128]{1,0:T(8,128)S(1)} %get-tuple-element.25), channel_id=1, source_target_pairs={{0,7},{1,6},{2,1},{3,0},{4,3},{5,2},{6,5},{7,4},{8,15},{9,14},{10,... | collective-permute-start | bytes 49160 | tf_op jit(solution)/shard_map/ppermute | solution.py:313
  6.1 1.6 %collective-permute-start.3 = (s32[32,128]{1,0:T(8,128)S(1)}, s32[32,128]{1,0:T(8,128)S(1)}, u32[]{:S(2)}, u32[]{:S(2)}) collective-permute-start(s32[32,128]{1,0:T(8,128)S(1)} %get-tuple-element.26), channel_id=1, source_target_pairs={{0,5},{1,4},{2,7},{3,6},{4,1},{5,0},{6,3},{7,2},{8,13},{9,12},{10,... | collective-permute-start | bytes 49160 | tf_op jit(solution)/shard_map/ppermute | solution.py:313
  7.8 0.9 %shard_map.57 = (s32[8,128]{1,0:T(8,128)S(1)}, bf16[256,1024]{1,0:T(8,128)(2,1)S(1)}) custom-call(s32[16]{0:T(128)} %assignment.3, s32[2,1024]{1,0:T(2,128)} %hint.1, s32[32,128]{1,0:T(8,128)S(1)} %get-tuple-element.21.after.refs_0_), custom_call_target="tpu_custom_call" | custom-call | tf_op jit(solution)/shard_map/pallas_call | solution.py:331
  8.7 0.0 collective-permute-done.1.refs_1_
  8.7 0.0 collective-permute-done.2.refs_2_
  8.7 0.6 %collective-permute-done.3.refs_3_ = s32[32,128]{1,0:T(8,128)S(1)} collective-permute-done((s32[32,128]{1,0:T(8,128)S(1)}, s32[32,128]{1,0:T(8,128)S(1)}, u32[]{:S(2)}, u32[]{:S(2)}) %collective-permute-start.3) | collective-permute-done | bytes 16416 | tf_op jit(solution)/shard_map/ppermute | solution.py:313
  9.4 2.7 %collective-permute-start.4 = (s32[40,128]{1,0:T(8,128)S(1)}, s32[40,128]{1,0:T(8,128)S(1)}, u32[]{:S(2)}, u32[]{:S(2)}) collective-permute-start(s32[40,128]{1,0:T(8,128)S(1)} %get-tuple-element.32), channel_id=1, source_target_pairs={{0,9},{1,8},{2,11},{3,10},{4,13},{5,12},{6,15},{7,14},{8,1},{9,0},... | collective-permute-start | bytes 61448 | tf_op jit(solution)/shard_map/ppermute | solution.py:313
  12.1 0.6 %shard_map.59 = (s32[8,128]{1,0:T(8,128)S(1)}, s32[8,128]{1,0:T(8,128)S(1)}, bf16[256,1024]{1,0:T(8,128)(2,1)S(1)}, bf16[128,256]{1,0:T(8,128)(2,1)S(1)}) custom-call(s32[8,128]{1,0:T(8,128)S(1)} %get-tuple-element.22.after.mask_in, bf16[256,1024]{1,0:T(8,128)(2,1)S(1)} %get-tuple-element.23.digits_in, s32[40,128]{1,0:T(8,128)S(1)} %get-tuple-element.27.part.own), custom_call_target="tpu_custom_call" | custom-call | tf_op jit(solution)/shard_map/pallas_call | solution.py:350
  12.7 0.9 %collective-permute-done.4.got = s32[40,128]{1,0:T(8,128)S(1)} collective-permute-done((s32[40,128]{1,0:T(8,128)S(1)}, s32[40,128]{1,0:T(8,128)S(1)}, u32[]{:S(2)}, u32[]{:S(2)}) %collective-permute-start.4) | collective-permute-done | bytes 20512 | tf_op jit(solution)/shard_map/ppermute | solution.py:313
  13.6 1.0 %shard_map.60 = f32[1,2,1024]{2,1,0:T(2,128)} custom-call(s32[8,128]{1,0:T(8,128)S(1)} %get-tuple-element.28.mask_in, bf16[256,1024]{1,0:T(8,128)(2,1)S(1)} %get-tuple-element.29.digits, s32[8,128]{1,0:T(8,128)S(1)} %get-tuple-element.30.change_in, bf16[128,256]{1,0:T(8,128)(2,1)S(1)} %get-tuple-element.31.own_matrix, ...), custom_call_target="tpu_custom_call" | custom-call | tf_op jit(solution)/shard_map/pallas_call | solution.py:382
  (2 shorter events, 0.0 us)
Async XLA Ops:
  1.0 1.4 %collective-permute-start = (s32[96,128]{1,0:T(8,128)S(1)}, s32[96,128]{1,0:T(8,128)S(1)}, u32[]{:S(2)}, u32[]{:S(2)}) collective-permute-start(s32[96,128]{1,0:T(8,128)S(1)} %get-tuple-element.20), channel_id=1, source_target_pairs={{0,1},{1,0},{2,3},{3,2},{4,5},{5,4},{6,7},{7,6},{8,9},{9,8},{10,11... | collective-permute-start | bytes 147464 | tf_op jit(solution)/shard_map/ppermute | solution.py:313
  2.4 6.3 %collective-permute-start.1 = (s32[32,128]{1,0:T(8,128)S(1)}, s32[32,128]{1,0:T(8,128)S(1)}, u32[]{:S(2)}, u32[]{:S(2)}) collective-permute-start(s32[32,128]{1,0:T(8,128)S(1)} %get-tuple-element.24), channel_id=1, source_target_pairs={{0,3},{1,2},{2,5},{3,4},{4,7},{5,6},{6,1},{7,0},{8,11},{9,10},{10,... | collective-permute-start | bytes 49160 | tf_op jit(solution)/shard_map/ppermute | solution.py:313
  5.1 3.6 %collective-permute-start.2 = (s32[32,128]{1,0:T(8,128)S(1)}, s32[32,128]{1,0:T(8,128)S(1)}, u32[]{:S(2)}, u32[]{:S(2)}) collective-permute-start(s32[32,128]{1,0:T(8,128)S(1)} %get-tuple-element.25), channel_id=1, source_target_pairs={{0,7},{1,6},{2,1},{3,0},{4,3},{5,2},{6,5},{7,4},{8,15},{9,14},{10,... | collective-permute-start | bytes 49160 | tf_op jit(solution)/shard_map/ppermute | solution.py:313
  6.1 3.2 %collective-permute-start.3 = (s32[32,128]{1,0:T(8,128)S(1)}, s32[32,128]{1,0:T(8,128)S(1)}, u32[]{:S(2)}, u32[]{:S(2)}) collective-permute-start(s32[32,128]{1,0:T(8,128)S(1)} %get-tuple-element.26), channel_id=1, source_target_pairs={{0,5},{1,4},{2,7},{3,6},{4,1},{5,0},{6,3},{7,2},{8,13},{9,12},{10,... | collective-permute-start | bytes 49160 | tf_op jit(solution)/shard_map/ppermute | solution.py:313
  9.4 4.2 %collective-permute-start.4 = (s32[40,128]{1,0:T(8,128)S(1)}, s32[40,128]{1,0:T(8,128)S(1)}, u32[]{:S(2)}, u32[]{:S(2)}) collective-permute-start(s32[40,128]{1,0:T(8,128)S(1)} %get-tuple-element.32), channel_id=1, source_target_pairs={{0,9},{1,8},{2,11},{3,10},{4,13},{5,12},{6,15},{7,14},{8,1},{9,0},... | collective-permute-start | bytes 61448 | tf_op jit(solution)/shard_map/ppermute | solution.py:313

commit v8 on v7

--- a/solution.py
+++ b/solution.py
@@ -16,20 +16,20 @@
 
 def stages_of(n):
     bits = [1 << k for k in range(n.bit_length() - 1)]
-    pair = [(3, 1), (7, 1), (5, 0)] if len(bits) > 2 else [(b | 1, 0) for b in bits[1:2]]
-    return [[(1, 0)]] + [pair] * (len(pair) > 0) + [[(b | 1, 0)] for b in bits[3:]]
+    square = [(5, 1), (3, 1), (7, 0)] if len(bits) > 2 else [(b | 1, 0) for b in bits[1:2]]
+    return [[(1, 0)]] + [square] * (len(square) > 0) + [[(b | 1, 0)] for b in bits[3:]]
 
 
 def moved(move, i):
-    mask, twist = move
-    if twist:
-        return i ^ mask ^ ((i & 2) << 1)
+    mask, turn = move
+    if turn:
+        return i ^ mask ^ (((i >> 1 ^ i >> 2) & 1) * 6)
     return i ^ mask
 
 
 def back(move):
-    mask, twist = move
-    return (mask ^ (mask & 2) << 1 if twist else mask, twist)
+    mask, turn = move
+    return (mask ^ 6 if turn else mask, turn)
 
 
 def follow(steps, i):

time: 14.8 us -> 14.8 us (level)
  waiting for transfers between devices: 2.39 us -> 2.24 us
    ppermute x5, waiting for transfers between devices: 2.39 us -> 2.24 us  [exchange(): return lax.ppermute(x, 'col', [(i, moved(move, i)) for i in range(n)])]
  transfers between devices with their start and end apart: 5 -> 5, of which waited for: 3 -> 3; matrix products, arithmetic and copies ran while one was open for 0% -> 0% of each run, Pallas kernels for 10% -> 11%
where the time goes in v8:
time: 14.8 us; the launch traced here: 14.5 us
  starting transfers between devices  8.68 us (59%)
  Pallas kernels  3.55 us (24%)
  waiting for transfers between devices  2.24 us (15%)
    ppermute x5, starting transfers between devices, exchange(): return lax.ppermute(x, 'col', [(i, moved(move, i)) for i in range(n)])  8.68 us
    ppermute x5, waiting for transfers between devices, exchange(): return lax.ppermute(x, 'col', [(i, moved(move, i)) for i in range(n)])  2.24 us
    pallas_call x1, Pallas kernels, on_device(): pl.pallas_call(functools.partial(answer_kernel, n, polys), out_shape=[plt...  1.02 us
    pallas_call x1, Pallas kernels, on_device(): pl.pallas_call(functools.partial(late_kernel, n, chunk) if halves else fu...  0.98 us
    pallas_call x1, Pallas kernels, digits_after(): pl.pallas_call(functools.partial(digit_kernel, polys), out_shape=[pltpu.V...  0.93 us
    pallas_call x1, Pallas kernels, on_device(): pl.pallas_call(functools.partial(early_kernel, n, chunk), out_shape=[pltp...  0.61 us
  transfers between devices with their start and end apart: 5, of which 3 were waited for; matrix products, arithmetic and copies ran while one was open for 0% of the time, Pallas kernels for 11%

profile of v8, /device:TPU:0, one launch (start us, length us, event | category | flops | bytes accessed | tf_op | source)
XLA Modules:
  0.0 14.5 jit_solution(16142431617586283234)
XLA Ops:
  0.0 1.0 %shard_map.55 = (s32[96,128]{1,0:T(8,128)S(1)}, s32[96,128]{1,0:T(8,128)S(1)}) custom-call(s32[16]{0:T(128)} %assignment.3, s32[16,2048]{1,0:T(8,128)} %refs_3_.1, s32[16,2048]{1,0:T(8,128)} %refs_3_.1, s32[16,2048]{1,0:T(8,128)} %refs_3_.1, s32[16,2048]{1,0:T(8,128)} %refs_3_.1, s32[8,16]{1,0:T(8,128)} %refs_4_.1, s32[8,512]{1,0:T(8,128)} %refs_5_.1), custom_call_target="tpu_custom_call" | custom-call | tf_op jit(solution)/shard_map/pallas_call | solution.py:319
  1.0 0.5 %collective-permute-start = (s32[96,128]{1,0:T(8,128)S(1)}, s32[96,128]{1,0:T(8,128)S(1)}, u32[]{:S(2)}, u32[]{:S(2)}) collective-permute-start(s32[96,128]{1,0:T(8,128)S(1)} %get-tuple-element.20), channel_id=1, source_target_pairs={{0,1},{1,0},{2,3},{3,2},{4,5},{5,4},{6,7},{7,6},{8,9},{9,8},{10,11... | collective-permute-start | bytes 147464 | tf_op jit(solution)/shard_map/ppermute | solution.py:313
  1.5 0.9 %collective-permute-done.refs_1_ = s32[96,128]{1,0:T(8,128)S(1)} collective-permute-done((s32[96,128]{1,0:T(8,128)S(1)}, s32[96,128]{1,0:T(8,128)S(1)}, u32[]{:S(2)}, u32[]{:S(2)}) %collective-permute-start) | collective-permute-done | bytes 49184 | tf_op jit(solution)/shard_map/ppermute | solution.py:313
  2.4 2.7 %collective-permute-start.1 = (s32[32,128]{1,0:T(8,128)S(1)}, s32[32,128]{1,0:T(8,128)S(1)}, u32[]{:S(2)}, u32[]{:S(2)}) collective-permute-start(s32[32,128]{1,0:T(8,128)S(1)} %get-tuple-element.24), channel_id=1, source_target_pairs={{0,5},{1,4},{2,1},{3,0},{4,7},{5,6},{6,3},{7,2},{8,13},{9,12},{10,... | collective-permute-start | bytes 49160 | tf_op jit(solution)/shard_map/ppermute | solution.py:313
  5.1 0.0 collective-permute-start.2
  5.1 2.7 %collective-permute-start.3 = (s32[32,128]{1,0:T(8,128)S(1)}, s32[32,128]{1,0:T(8,128)S(1)}, u32[]{:S(2)}, u32[]{:S(2)}) collective-permute-start(s32[32,128]{1,0:T(8,128)S(1)} %get-tuple-element.26), channel_id=1, source_target_pairs={{0,7},{1,6},{2,5},{3,4},{4,3},{5,2},{6,1},{7,0},{8,15},{9,14},{10,... | collective-permute-start | bytes 49160 | tf_op jit(solution)/shard_map/ppermute | solution.py:313
  7.8 0.9 %shard_map.57 = (s32[8,128]{1,0:T(8,128)S(1)}, bf16[256,1024]{1,0:T(8,128)(2,1)S(1)}) custom-call(s32[16]{0:T(128)} %assignment.3, s32[2,1024]{1,0:T(2,128)} %hint.1, s32[32,128]{1,0:T(8,128)S(1)} %get-tuple-element.21.after.refs_0_), custom_call_target="tpu_custom_call" | custom-call | tf_op jit(solution)/shard_map/pallas_call | solution.py:331
  8.8 0.0 collective-permute-done.1.refs_1_
  8.8 0.0 collective-permute-done.2.refs_2_
  8.8 0.5 %collective-permute-done.3.refs_3_ = s32[32,128]{1,0:T(8,128)S(1)} collective-permute-done((s32[32,128]{1,0:T(8,128)S(1)}, s32[32,128]{1,0:T(8,128)S(1)}, u32[]{:S(2)}, u32[]{:S(2)}) %collective-permute-start.3) | collective-permute-done | bytes 16416 | tf_op jit(solution)/shard_map/ppermute | solution.py:313
  9.3 2.8 %collective-permute-start.4 = (s32[40,128]{1,0:T(8,128)S(1)}, s32[40,128]{1,0:T(8,128)S(1)}, u32[]{:S(2)}, u32[]{:S(2)}) collective-permute-start(s32[40,128]{1,0:T(8,128)S(1)} %get-tuple-element.32), channel_id=1, source_target_pairs={{0,9},{1,8},{2,11},{3,10},{4,13},{5,12},{6,15},{7,14},{8,1},{9,0},... | collective-permute-start | bytes 61448 | tf_op jit(solution)/shard_map/ppermute | solution.py:313
  12.1 0.6 %shard_map.59 = (s32[8,128]{1,0:T(8,128)S(1)}, s32[8,128]{1,0:T(8,128)S(1)}, bf16[256,1024]{1,0:T(8,128)(2,1)S(1)}, bf16[128,256]{1,0:T(8,128)(2,1)S(1)}) custom-call(s32[8,128]{1,0:T(8,128)S(1)} %get-tuple-element.22.after.mask_in, bf16[256,1024]{1,0:T(8,128)(2,1)S(1)} %get-tuple-element.23.digits_in, s32[40,128]{1,0:T(8,128)S(1)} %get-tuple-element.27.part.own), custom_call_target="tpu_custom_call" | custom-call | tf_op jit(solution)/shard_map/pallas_call | solution.py:350
  12.7 0.9 %collective-permute-done.4.got = s32[40,128]{1,0:T(8,128)S(1)} collective-permute-done((s32[40,128]{1,0:T(8,128)S(1)}, s32[40,128]{1,0:T(8,128)S(1)}, u32[]{:S(2)}, u32[]{:S(2)}) %collective-permute-start.4) | collective-permute-done | bytes 20512 | tf_op jit(solution)/shard_map/ppermute | solution.py:313
  13.5 1.0 %shard_map.60 = f32[1,2,1024]{2,1,0:T(2,128)} custom-call(s32[8,128]{1,0:T(8,128)S(1)} %get-tuple-element.28.mask_in, bf16[256,1024]{1,0:T(8,128)(2,1)S(1)} %get-tuple-element.29.digits, s32[8,128]{1,0:T(8,128)S(1)} %get-tuple-element.30.change_in, bf16[128,256]{1,0:T(8,128)(2,1)S(1)} %get-tuple-element.31.own_matrix, ...), custom_call_target="tpu_custom_call" | custom-call | tf_op jit(solution)/shard_map/pallas_call | solution.py:382
  (2 shorter events, 0.0 us)
Async XLA Ops:
  1.0 1.4 %collective-permute-start = (s32[96,128]{1,0:T(8,128)S(1)}, s32[96,128]{1,0:T(8,128)S(1)}, u32[]{:S(2)}, u32[]{:S(2)}) collective-permute-start(s32[96,128]{1,0:T(8,128)S(1)} %get-tuple-element.20), channel_id=1, source_target_pairs={{0,1},{1,0},{2,3},{3,2},{4,5},{5,4},{6,7},{7,6},{8,9},{9,8},{10,11... | collective-permute-start | bytes 147464 | tf_op jit(solution)/shard_map/ppermute | solution.py:313
  2.4 6.3 %collective-permute-start.1 = (s32[32,128]{1,0:T(8,128)S(1)}, s32[32,128]{1,0:T(8,128)S(1)}, u32[]{:S(2)}, u32[]{:S(2)}) collective-permute-start(s32[32,128]{1,0:T(8,128)S(1)} %get-tuple-element.24), channel_id=1, source_target_pairs={{0,5},{1,4},{2,1},{3,0},{4,7},{5,6},{6,3},{7,2},{8,13},{9,12},{10,... | collective-permute-start | bytes 49160 | tf_op jit(solution)/shard_map/ppermute | solution.py:313
  5.1 3.6 %collective-permute-start.2 = (s32[32,128]{1,0:T(8,128)S(1)}, s32[32,128]{1,0:T(8,128)S(1)}, u32[]{:S(2)}, u32[]{:S(2)}) collective-permute-start(s32[32,128]{1,0:T(8,128)S(1)} %get-tuple-element.25), channel_id=1, source_target_pairs={{0,3},{1,2},{2,7},{3,6},{4,1},{5,0},{6,5},{7,4},{8,11},{9,10},{10,... | collective-permute-start | bytes 49160 | tf_op jit(solution)/shard_map/ppermute | solution.py:313
  5.1 4.1 %collective-permute-start.3 = (s32[32,128]{1,0:T(8,128)S(1)}, s32[32,128]{1,0:T(8,128)S(1)}, u32[]{:S(2)}, u32[]{:S(2)}) collective-permute-start(s32[32,128]{1,0:T(8,128)S(1)} %get-tuple-element.26), channel_id=1, source_target_pairs={{0,7},{1,6},{2,5},{3,4},{4,3},{5,2},{6,1},{7,0},{8,15},{9,14},{10,... | collective-permute-start | bytes 49160 | tf_op jit(solution)/shard_map/ppermute | solution.py:313
  9.3 4.3 %collective-permute-start.4 = (s32[40,128]{1,0:T(8,128)S(1)}, s32[40,128]{1,0:T(8,128)S(1)}, u32[]{:S(2)}, u32[]{:S(2)}) collective-permute-start(s32[40,128]{1,0:T(8,128)S(1)} %get-tuple-element.32), channel_id=1, source_target_pairs={{0,9},{1,8},{2,11},{3,10},{4,13},{5,12},{6,15},{7,14},{8,1},{9,0},... | collective-permute-start | bytes 61448 | tf_op jit(solution)/shard_map/ppermute | solution.py:313

commit v9 on v8

--- a/solution.py
+++ b/solution.py
@@ -61,7 +61,7 @@
     words = queries[...]
     bytes_ = [jnp.bitwise_and(jnp.right_shift(words, 8 * j), 255) for j in range(4)]
     lhs = jnp.concatenate(bytes_, axis=0).astype(jnp.float32).astype(jnp.bfloat16)
-    rhs = jnp.concatenate([part[...] for part in database], axis=1).astype(jnp.float32).astype(jnp.bfloat16)
+    rhs = jnp.concatenate([part[...].astype(jnp.float32).astype(jnp.bfloat16) for part in database], axis=1)
     sums = jnp.dot(lhs, rhs, preferred_element_type=jnp.float32).astype(jnp.int32)
     partial = sums[:clients]
     for j in range(1, 4):
@@ -246,10 +246,9 @@
         mask = mask + change[0]
         value = value + automorph(value, level) + change[1]
         level += 1
-    for p, words in enumerate((mask, value)):
-        scaled = words.astype(jnp.float32) * 2.0**-32
-        for b in range(cycle_blocks):
-            packed[0, p : p + 1, b * LANES : (b + 1) * LANES] = scaled[b : b + 1, :]
+    scaled = [words.astype(jnp.float32) * 2.0**-32 for words in (mask, value)]
+    for b in range(cycle_blocks):
+        packed[0, :, b * LANES : (b + 1) * LANES] = jnp.concatenate([words[b : b + 1, :] for words in scaled], axis=0)
 
 
 def sum_answers(parts, cycle_blocks):

time: 14.8 us -> 14.8 us (level)
  no operation moved by 1% of the time
where the time goes in v9:
time: 14.8 us; the launch traced here: 14.5 us
  starting transfers between devices  8.68 us (59%)
  Pallas kernels  3.55 us (24%)
  waiting for transfers between devices  2.24 us (15%)
    ppermute x5, starting transfers between devices, exchange(): return lax.ppermute(x, 'col', [(i, moved(move, i)) for i in range(n)])  8.68 us
    ppermute x5, waiting for transfers between devices, exchange(): return lax.ppermute(x, 'col', [(i, moved(move, i)) for i in range(n)])  2.24 us
    pallas_call x1, Pallas kernels, on_device(): pl.pallas_call(functools.partial(answer_kernel, n, polys), out_shape=[plt...  1.02 us
    pallas_call x1, Pallas kernels, on_device(): pl.pallas_call(functools.partial(late_kernel, n, chunk) if halves else fu...  0.98 us
    pallas_call x1, Pallas kernels, digits_after(): pl.pallas_call(functools.partial(digit_kernel, polys), out_shape=[pltpu.V...  0.93 us
    pallas_call x1, Pallas kernels, on_device(): pl.pallas_call(functools.partial(early_kernel, n, chunk), out_shape=[pltp...  0.61 us
  transfers between devices with their start and end apart: 5, of which 3 were waited for; matrix products, arithmetic and copies ran while one was open for 0% of the time, Pallas kernels for 11%

profile of v9, /device:TPU:0, one launch (start us, length us, event | category | flops | bytes accessed | tf_op | source)
XLA Modules:
  0.0 14.5 jit_solution(7218277916642897841)
XLA Ops:
  0.0 1.0 %shard_map.55 = (s32[96,128]{1,0:T(8,128)S(1)}, s32[96,128]{1,0:T(8,128)S(1)}) custom-call(s32[16]{0:T(128)} %assignment.3, s32[16,2048]{1,0:T(8,128)} %refs_3_.1, s32[16,2048]{1,0:T(8,128)} %refs_3_.1, s32[16,2048]{1,0:T(8,128)} %refs_3_.1, s32[16,2048]{1,0:T(8,128)} %refs_3_.1, s32[8,16]{1,0:T(8,128)} %refs_4_.1, s32[8,512]{1,0:T(8,128)} %refs_5_.1), custom_call_target="tpu_custom_call" | custom-call | tf_op jit(solution)/shard_map/pallas_call | solution.py:318
  1.0 0.5 %collective-permute-start = (s32[96,128]{1,0:T(8,128)S(1)}, s32[96,128]{1,0:T(8,128)S(1)}, u32[]{:S(2)}, u32[]{:S(2)}) collective-permute-start(s32[96,128]{1,0:T(8,128)S(1)} %get-tuple-element.20), channel_id=1, source_target_pairs={{0,1},{1,0},{2,3},{3,2},{4,5},{5,4},{6,7},{7,6},{8,9},{9,8},{10,11... | collective-permute-start | bytes 147464 | tf_op jit(solution)/shard_map/ppermute | solution.py:312
  1.5 0.9 %collective-permute-done.refs_1_ = s32[96,128]{1,0:T(8,128)S(1)} collective-permute-done((s32[96,128]{1,0:T(8,128)S(1)}, s32[96,128]{1,0:T(8,128)S(1)}, u32[]{:S(2)}, u32[]{:S(2)}) %collective-permute-start) | collective-permute-done | bytes 49184 | tf_op jit(solution)/shard_map/ppermute | solution.py:312
  2.4 2.7 %collective-permute-start.1 = (s32[32,128]{1,0:T(8,128)S(1)}, s32[32,128]{1,0:T(8,128)S(1)}, u32[]{:S(2)}, u32[]{:S(2)}) collective-permute-start(s32[32,128]{1,0:T(8,128)S(1)} %get-tuple-element.24), channel_id=1, source_target_pairs={{0,5},{1,4},{2,1},{3,0},{4,7},{5,6},{6,3},{7,2},{8,13},{9,12},{10,... | collective-permute-start | bytes 49160 | tf_op jit(solution)/shard_map/ppermute | solution.py:312
  5.1 0.0 collective-permute-start.2
  5.1 2.7 %collective-permute-start.3 = (s32[32,128]{1,0:T(8,128)S(1)}, s32[32,128]{1,0:T(8,128)S(1)}, u32[]{:S(2)}, u32[]{:S(2)}) collective-permute-start(s32[32,128]{1,0:T(8,128)S(1)} %get-tuple-element.26), channel_id=1, source_target_pairs={{0,7},{1,6},{2,5},{3,4},{4,3},{5,2},{6,1},{7,0},{8,15},{9,14},{10,... | collective-permute-start | bytes 49160 | tf_op jit(solution)/shard_map/ppermute | solution.py:312
  7.8 0.9 %shard_map.57 = (s32[8,128]{1,0:T(8,128)S(1)}, bf16[256,1024]{1,0:T(8,128)(2,1)S(1)}) custom-call(s32[16]{0:T(128)} %assignment.3, s32[2,1024]{1,0:T(2,128)} %hint.1, s32[32,128]{1,0:T(8,128)S(1)} %get-tuple-element.21.after.refs_0_), custom_call_target="tpu_custom_call" | custom-call | tf_op jit(solution)/shard_map/pallas_call | solution.py:330
  8.8 0.0 collective-permute-done.1.refs_1_
  8.8 0.0 collective-permute-done.2.refs_2_
  8.8 0.5 %collective-permute-done.3.refs_3_ = s32[32,128]{1,0:T(8,128)S(1)} collective-permute-done((s32[32,128]{1,0:T(8,128)S(1)}, s32[32,128]{1,0:T(8,128)S(1)}, u32[]{:S(2)}, u32[]{:S(2)}) %collective-permute-start.3) | collective-permute-done | bytes 16416 | tf_op jit(solution)/shard_map/ppermute | solution.py:312
  9.3 2.8 %collective-permute-start.4 = (s32[40,128]{1,0:T(8,128)S(1)}, s32[40,128]{1,0:T(8,128)S(1)}, u32[]{:S(2)}, u32[]{:S(2)}) collective-permute-start(s32[40,128]{1,0:T(8,128)S(1)} %get-tuple-element.32), channel_id=1, source_target_pairs={{0,9},{1,8},{2,11},{3,10},{4,13},{5,12},{6,15},{7,14},{8,1},{9,0},... | collective-permute-start | bytes 61448 | tf_op jit(solution)/shard_map/ppermute | solution.py:312
  12.1 0.6 %shard_map.59 = (s32[8,128]{1,0:T(8,128)S(1)}, s32[8,128]{1,0:T(8,128)S(1)}, bf16[256,1024]{1,0:T(8,128)(2,1)S(1)}, bf16[128,256]{1,0:T(8,128)(2,1)S(1)}) custom-call(s32[8,128]{1,0:T(8,128)S(1)} %get-tuple-element.22.after.mask_in, bf16[256,1024]{1,0:T(8,128)(2,1)S(1)} %get-tuple-element.23.digits_in, s32[40,128]{1,0:T(8,128)S(1)} %get-tuple-element.27.part.own), custom_call_target="tpu_custom_call" | custom-call | tf_op jit(solution)/shard_map/pallas_call | solution.py:349
  12.7 0.9 %collective-permute-done.4.got = s32[40,128]{1,0:T(8,128)S(1)} collective-permute-done((s32[40,128]{1,0:T(8,128)S(1)}, s32[40,128]{1,0:T(8,128)S(1)}, u32[]{:S(2)}, u32[]{:S(2)}) %collective-permute-start.4) | collective-permute-done | bytes 20512 | tf_op jit(solution)/shard_map/ppermute | solution.py:312
  13.5 1.0 %shard_map.60 = f32[1,2,1024]{2,1,0:T(2,128)} custom-call(s32[8,128]{1,0:T(8,128)S(1)} %get-tuple-element.28.mask_in, bf16[256,1024]{1,0:T(8,128)(2,1)S(1)} %get-tuple-element.29.digits, s32[8,128]{1,0:T(8,128)S(1)} %get-tuple-element.30.change_in, bf16[128,256]{1,0:T(8,128)(2,1)S(1)} %get-tuple-element.31.own_matrix, ...), custom_call_target="tpu_custom_call" | custom-call | tf_op jit(solution)/shard_map/pallas_call | solution.py:381
  (2 shorter events, 0.0 us)
Async XLA Ops:
  1.0 1.4 %collective-permute-start = (s32[96,128]{1,0:T(8,128)S(1)}, s32[96,128]{1,0:T(8,128)S(1)}, u32[]{:S(2)}, u32[]{:S(2)}) collective-permute-start(s32[96,128]{1,0:T(8,128)S(1)} %get-tuple-element.20), channel_id=1, source_target_pairs={{0,1},{1,0},{2,3},{3,2},{4,5},{5,4},{6,7},{7,6},{8,9},{9,8},{10,11... | collective-permute-start | bytes 147464 | tf_op jit(solution)/shard_map/ppermute | solution.py:312
  2.4 6.3 %collective-permute-start.1 = (s32[32,128]{1,0:T(8,128)S(1)}, s32[32,128]{1,0:T(8,128)S(1)}, u32[]{:S(2)}, u32[]{:S(2)}) collective-permute-start(s32[32,128]{1,0:T(8,128)S(1)} %get-tuple-element.24), channel_id=1, source_target_pairs={{0,5},{1,4},{2,1},{3,0},{4,7},{5,6},{6,3},{7,2},{8,13},{9,12},{10,... | collective-permute-start | bytes 49160 | tf_op jit(solution)/shard_map/ppermute | solution.py:312
  5.1 3.6 %collective-permute-start.2 = (s32[32,128]{1,0:T(8,128)S(1)}, s32[32,128]{1,0:T(8,128)S(1)}, u32[]{:S(2)}, u32[]{:S(2)}) collective-permute-start(s32[32,128]{1,0:T(8,128)S(1)} %get-tuple-element.25), channel_id=1, source_target_pairs={{0,3},{1,2},{2,7},{3,6},{4,1},{5,0},{6,5},{7,4},{8,11},{9,10},{10,... | collective-permute-start | bytes 49160 | tf_op jit(solution)/shard_map/ppermute | solution.py:312
  5.1 4.1 %collective-permute-start.3 = (s32[32,128]{1,0:T(8,128)S(1)}, s32[32,128]{1,0:T(8,128)S(1)}, u32[]{:S(2)}, u32[]{:S(2)}) collective-permute-start(s32[32,128]{1,0:T(8,128)S(1)} %get-tuple-element.26), channel_id=1, source_target_pairs={{0,7},{1,6},{2,5},{3,4},{4,3},{5,2},{6,1},{7,0},{8,15},{9,14},{10,... | collective-permute-start | bytes 49160 | tf_op jit(solution)/shard_map/ppermute | solution.py:312
  9.3 4.3 %collective-permute-start.4 = (s32[40,128]{1,0:T(8,128)S(1)}, s32[40,128]{1,0:T(8,128)S(1)}, u32[]{:S(2)}, u32[]{:S(2)}) collective-permute-start(s32[40,128]{1,0:T(8,128)S(1)} %get-tuple-element.32), channel_id=1, source_target_pairs={{0,9},{1,8},{2,11},{3,10},{4,13},{5,12},{6,15},{7,14},{8,1},{9,0},... | collective-permute-start | bytes 61448 | tf_op jit(solution)/shard_map/ppermute | solution.py:312
